TPU v7x, 256 devices: a whole 4x4x8 slice. The times are simulated.
256 devices in a mesh: gx: 8 (over z_hi, core), gy: 8 (over y, z_lo), gz: 4 (over x).
Axes of the slice: x: 4, y: 4, z: 8 (z_hi: 4, z_lo: 2; z = z_hi * 2 + z_lo), core: 2. Of those that a mesh axis runs over, the one named last changes fastest.
Arguments:
- displacement: float32 [3, 64, 128, 512], P(None, 'gx', 'gy', 'gz'), may hold values from -0.16 to 0.16
- velocity: float32 [3, 64, 128, 512], P(None, 'gx', 'gy', 'gz'), may hold values from -1.2 to 1.2
- stiffness: float32 [64, 128, 512], P('gx', 'gy', 'gz'), may hold values from 0.5 to 2
- broken: int32 [61, 64, 128, 512], P(None, 'gx', 'gy', 'gz'), may hold values 0 or 1
- borehole_id: int32 [64, 128, 512], P('gx', 'gy', 'gz'), may hold values from 0 to 7
- flags: int32 [64, 128, 512], P('gx', 'gy', 'gz'), may hold values 0 or 1
- pressure: float32 [8], replicated, may hold values from 0.5 to 4
Outputs:
- displacement_out: float32 [3, 64, 128, 512], P(None, 'gx', 'gy', 'gz')
- velocity_out: float32 [3, 64, 128, 512], P(None, 'gx', 'gy', 'gz')
- accel_out: float32 [3, 64, 128, 512], P(None, 'gx', 'gy', 'gz')
All inputs are finite; a program needn't handle non-finite values. No bound on the sum of `broken` or of `flags` on one device may be relied on, other than what follows from the above.
Results may differ from a plain program's by a relative error of at most 0.00002.
Values sent between devices are 32-bit elements; how exact they have to be, the bound alone decides.
No kernel may reach another device: no remote copies, remote signals or barrier semaphores. Data moves between devices by JAX's collectives and lax.ppermute only.
A program may use at most 192 MiB of HBM per device.

v0:
```python
import functools
import math

import jax
import jax.numpy as jnp
from jax import lax
from jax.experimental import pallas as pl
from jax.experimental.pallas import tpu as pltpu
from jax.sharding import PartitionSpec as P

STEPS = 2
C_BOND = 3.0
DT_STEP = 0.04
REACH = 3
NEAR = 2
LANES = 128
SLOT = 16
PAD = 8
UNROLL = 2
UNROLL_FILL = 2
FIRST = 8
HALF_DT = 0.5 * DT_STEP


def half_offsets():
    result = []
    for step_x in range(0, 4):
        for step_y in range(-3, 4):
            for step_z in range(-3, 4):
                square = step_x * step_x + step_y * step_y + step_z * step_z
                if square == 0 or square > 9:
                    continue
                if step_x > 0 or (step_x == 0 and (step_y > 0 or (step_y == 0 and step_z > 0))):
                    result.append((step_x, step_y, step_z))
    return result


OFFSETS = half_offsets()
BONDS = {step: [] for step in range(-REACH, REACH + 1)}
for _plane, (_a, _b, _c) in enumerate(OFFSETS):
    BONDS[_a].append((_b, _c, _plane, True))
    BONDS[-_a].append((-_b, -_c, _plane, False))


def inner_layers(step, extent):
    return max(0, -step), min(extent, extent - step)


def outer_layers(step, extent):
    return (extent - step, extent) if step > 0 else (0, -step)


STEPS_ALL = list(range(-REACH, REACH + 1))
STEPS_OUT = [step for step in STEPS_ALL if step != 0]


def tiled_bonds(step, tiles):
    early, late = [], []
    for tile in range(tiles):
        for bond in BONDS[step]:
            low, high = 8 * tile + bond[0], 8 * tile + 8 + bond[0]
            (early if low >= 0 and high <= 8 * tiles else late).append((tile, *bond))
    return early, late


def inner_plan(extent, late):
    plan, total = [], 0
    for step in STEPS_ALL:
        bonds = tiled_bonds(step, extent[1] // 8)[int(late)]
        first, last = inner_layers(step, extent[0])
        plan.append((step, first, last, bonds, total))
        total += (last - first) * len(bonds)
    return plan, total


def outer_plan(extent):
    plan, total = [], 0
    for step in STEPS_OUT:
        bonds = [(tile, *bond) for tile in range(extent[1] // 8) for bond in BONDS[step]]
        first, last = outer_layers(step, extent[0])
        plan.append((step, first, last, bonds, total))
        total += (last - first) * len(bonds)
    return plan, total


def reach_beside(distance):
    return max(max(abs(b), abs(c)) for a, b, c in OFFSETS if a >= distance)


def x_span(distance, size_y):
    return REACH - reach_beside(distance), REACH + size_y + reach_beside(distance)


def x_place(field, distance, size_y):
    lengths = [high - low for low, high in (x_span(far, size_y) for far in (3, 2, 1))]
    return field * sum(lengths) + sum(lengths[: REACH - distance])


def round_up(count):
    return (count + 7) // 8 * 8


def running(amounts):
    places, total = {}, 0
    for plane, amount in amounts:
        places[plane] = total
        total += amount
    return places, total


Z_UP, Z_UP_COUNT = running([(k, c) for k, (a, b, c) in enumerate(OFFSETS) if c > 0])
Z_DOWN, Z_DOWN_COUNT = running([(k, -c) for k, (a, b, c) in enumerate(OFFSETS) if c < 0])
Y_UP, Y_UP_COUNT = running([(k, b) for k, (a, b, c) in enumerate(OFFSETS) if b > 0])
Y_DOWN, Y_DOWN_COUNT = running([(k, -b) for k, (a, b, c) in enumerate(OFFSETS) if b < 0])
X_UP, X_UP_COUNT = running([(k, a) for k, (a, b, c) in enumerate(OFFSETS) if a > 0])
XY_UP, XY_UP_COUNT = running([(k, a * abs(b)) for k, (a, b, c) in enumerate(OFFSETS) if a * abs(b) > 0])


def lanes_like(value):
    return lax.broadcasted_iota(jnp.int32, value.shape, value.ndim - 1)


def rolled(value, shift):
    shift = shift % LANES
    return value if shift == 0 else pltpu.roll(value, shift, value.ndim - 1)


def beside_columns(low_pack, high_pack, lane_of, high_lanes=0):
    lanes = lanes_like(low_pack)
    return jnp.where(
        lanes < REACH,
        rolled(high_pack, -lane_of - high_lanes),
        rolled(low_pack, LANES - REACH - lane_of),
    )


def moved(main, beside, step):
    if step == 0:
        return main
    lanes = lanes_like(main)
    if step > 0:
        return rolled(jnp.where(lanes < step, beside, main), -step)
    return rolled(jnp.where(lanes >= LANES + step, beside, main), -step)


def pack_columns(field_of, count, extent, height):
    lanes = lax.broadcasted_iota(jnp.int32, (height, LANES), 1)
    up = jnp.zeros((height, LANES), jnp.float32)
    down = up
    for layer in range(extent):
        for field in range(count):
            lane_of = layer * SLOT + field * REACH
            value = field_of(field, layer)
            here = (lanes >= lane_of) & (lanes < lane_of + REACH)
            up = jnp.where(here, rolled(value, lane_of - (LANES - REACH)), up)
            down = jnp.where(here, rolled(value, lane_of), down)
    return up, down


def kept(flag, value):
    return jnp.where(flag > 0, value, 0.0)


def start_kernel(
    extent, pressure_in, motion_in, stiffness_in, borehole_in, flags_in, broken_in,
    motion, stiffness, pore, z_up, z_down, rows_up, rows_down, x_up,
    broken, pressure, borehole, flags, field_sems, layer_sems,
):
    size_x, size_y, _ = extent
    pairs = (
        (pressure_in, pressure), (borehole_in, borehole), (flags_in, flags),
        (motion_in, motion), (stiffness_in, stiffness),
    )
    copies = [
        pltpu.make_async_copy(source, target, field_sems.at[place])
        for place, (source, target) in enumerate(pairs)
    ]

    def layer_copy(layer):
        return pltpu.make_async_copy(
            broken_in.at[:, layer], broken.at[:, layer], layer_sems.at[layer]
        )

    for copy in copies:
        copy.start()
    for layer in range(size_x):
        layer_copy(layer).start()
    for copy in copies:
        copy.wait()
    ids = borehole[...]
    level = jnp.zeros(ids.shape, jnp.float32)
    for label in range(pressure.shape[0]):
        level = jnp.where(ids == label, pressure[label], level)
    pore[...] = flags[...].astype(jnp.float32) * level

    def field_of(field, layer):
        if field < 3:
            return motion[field, layer]
        return stiffness[layer] if field == 3 else pore[layer]

    up, down = pack_columns(field_of, 5, size_x, size_y)
    z_up[0:size_y] = up
    z_down[0:size_y] = down

    def one_layer(layer, carry):
        layer_copy(layer).wait()
        lanes = lax.broadcasted_iota(jnp.int32, (size_y, LANES), 1)
        rows = pl.ds(size_y + layer * size_y, size_y)
        up = jnp.zeros((size_y, LANES), jnp.float32)
        down = up
        for plane, (_, _, c) in enumerate(OFFSETS):
            if c > 0:
                at = Z_UP[plane]
                value = broken[plane, layer].astype(jnp.float32)
                up = jnp.where((lanes >= at) & (lanes < at + c), rolled(value, at + c), up)
            if c < 0:
                at = Z_DOWN[plane]
                value = broken[plane, layer].astype(jnp.float32)
                down = jnp.where((lanes >= at) & (lanes < at - c), rolled(value, at), down)
        z_up[rows] = up
        z_down[rows] = down
        return carry

    lax.fori_loop(0, size_x, one_layer, 0)
    for plane, (a, _, _) in enumerate(OFFSETS):
        for layer in range(a):
            at = (X_UP[plane] + layer) * size_y
            x_up[at : at + size_y] = broken[plane, size_x - a + layer].astype(jnp.float32)
    for plane, (_, b, _) in enumerate(OFFSETS):
        for layer in range(size_x):
            if b > 0:
                at = PAD + Y_UP[plane] * size_x + layer * b
                rows_up[at : at + b] = broken[plane, layer, size_y - b : size_y].astype(jnp.float32)
            if b < 0:
                at = PAD + Y_DOWN[plane] * size_x - layer * b
                rows_down[at : at - b] = broken[plane, layer, 0:-b].astype(jnp.float32)


def copy_y_rows(field_of, count, extent, low_pack, high_pack, y_up, y_down):
    size_x, size_y, _ = extent
    for field in range(count):
        for layer in range(size_x):
            at = (field * size_x + layer) * REACH
            y_up[at : at + REACH] = field_of(field, layer, slice(size_y - REACH, size_y))
            y_down[at : at + REACH] = field_of(field, layer, slice(0, REACH))
    at = count * size_x * REACH
    for pack in (low_pack, high_pack):
        y_up[at : at + REACH] = pack[size_y - REACH : size_y]
        y_down[at : at + REACH] = pack[0:REACH]
        at += REACH
    return at


def y_rows_kernel(extent, edges, motion, z_low, z_high, y_up, y_down):
    size_y = extent[1]
    low_pack = kept(edges[0], z_low[0:size_y])
    high_pack = kept(edges[1], z_high[0:size_y])
    copy_y_rows(
        lambda field, layer, rows: motion[field, layer, rows],
        3, extent, low_pack, high_pack, y_up, y_down,
    )


def y_rows_first_kernel(extent, edges, motion, stiffness, pore, z_low, z_high, y_up, y_down):
    size_x, size_y, _ = extent
    low_pack = kept(edges[0], z_low[0:size_y])
    high_pack = kept(edges[1], z_high[0:size_y])

    def field_of(field, layer, rows):
        if field < 3:
            return motion[field, layer, rows]
        return stiffness[layer, rows] if field == 3 else pore[layer, rows]

    base = copy_y_rows(field_of, 5, extent, low_pack, high_pack, y_up, y_down)
    for order, pack in enumerate((z_low, z_high)):
        for layer in range(size_x):
            first = size_y + layer * size_y
            at = base + (order * size_x + layer) * REACH
            y_up[at : at + REACH] = pack[first + size_y - REACH : first + size_y]
            y_down[at : at + REACH] = pack[first : first + REACH]


def widen(target, low_rows, middle, high_rows):
    size_y = middle.shape[0]
    target[0:REACH] = low_rows
    target[REACH : REACH + size_y] = middle
    target[REACH + size_y : 2 * REACH + size_y] = high_rows
    height = target.shape[0]
    target[2 * REACH + size_y : height] = jnp.zeros((height - 2 * REACH - size_y, LANES), jnp.float32)


def widen_fields(edges, field_of, count, extent, z_low, z_high, y_low, y_high, target, wide_pack):
    size_x, size_y, _ = extent
    for field in range(count):
        for layer in range(size_x):
            at = (field * size_x + layer) * REACH
            widen(
                target(field).at[layer],
                kept(edges[2], y_low[at : at + REACH]),
                field_of(field, layer),
                kept(edges[3], y_high[at : at + REACH]),
            )
    at = count * size_x * REACH
    for order, pack in enumerate((z_low, z_high)):
        widen(
            wide_pack.at[order],
            kept(edges[2], y_low[at : at + REACH]),
            kept(edges[order], pack[0:size_y]),
            kept(edges[3], y_high[at : at + REACH]),
        )
        at += REACH
    return at


def copy_x_layers(count, extent, target, wide_pack, x_up, x_down):
    size_x, size_y, _ = extent
    height = wide_pack.shape[1]
    for field in range(count):
        for distance in (3, 2, 1):
            low, high = x_span(distance, size_y)
            at = x_place(field, distance, size_y)
            x_up[at : at + high - low] = target(field)[size_x - distance, low:high]
            x_down[at : at + high - low] = target(field)[distance - 1, low:high]
    at = x_place(count, REACH, size_y)
    low_pack, high_pack = wide_pack[0], wide_pack[1]
    half = lanes_like(low_pack) < LANES // 2
    other = rolled(high_pack, LANES // 2)
    x_up[at : at + height] = jnp.where(half, other, low_pack)
    x_down[at : at + height] = jnp.where(half, low_pack, other)
    return at + height


def x_layers_kernel(
    extent, edges, motion, z_low, z_high, y_low, y_high, x_up, x_down, wide, wide_pack
):
    widen_fields(
        edges, lambda field, layer: motion[field, layer],
        3, extent, z_low, z_high, y_low, y_high, lambda field: wide.at[field], wide_pack,
    )
    copy_x_layers(3, extent, lambda field: wide.at[field], wide_pack, x_up, x_down)


def x_layers_first_kernel(
    extent, edges, motion, stiffness, pore, z_low, z_high, y_low, y_high, rows_low, rows_high,
    wide_static, wide_pack, wide_broken, x_up, x_down, wide,
):
    size_x, size_y, _ = extent

    def field_of(field, layer):
        if field < 3:
            return motion[field, layer]
        return stiffness[layer] if field == 3 else pore[layer]

    def target(field):
        return wide.at[field] if field < 3 else wide_static.at[field - 3]

    base = widen_fields(
        edges, field_of, 5, extent, z_low, z_high, y_low, y_high, target, wide_pack
    )
    for order, pack in enumerate((z_low, z_high)):
        for layer in range(size_x):
            first = size_y + layer * size_y
            at = base + (order * size_x + layer) * REACH
            widen(
                wide_broken.at[order, layer],
                y_low[at : at + REACH],
                pack[first : first + size_y],
                y_high[at : at + REACH],
            )
    at = copy_x_layers(4, extent, target, wide_pack, x_up, x_down)
    height = wide.shape[2]
    x_up[at : at + size_y] = pore[size_x - 1]
    x_down[at : at + size_y] = pore[0]
    at += size_y
    for order in range(2):
        for layer in range(NEAR):
            x_up[at : at + height] = wide_broken[order, size_x - NEAR + layer]
            at += height
    for plane, (a, b, _) in enumerate(OFFSETS):
        if a * b == 0:
            continue
        rows, many = abs(b), a * abs(b)
        source = rows_low if b > 0 else rows_high
        first = PAD + (Y_UP if b > 0 else Y_DOWN)[plane] * size_x + (size_x - a) * rows
        x_up[at + XY_UP[plane] : at + XY_UP[plane] + many] = source[first : first + many]


def each_shift(main, beside, add_step, reach=REACH):
    for step in range(-reach, reach + 1):
        value = moved(main, beside, step)
        yield step + REACH, value + float(step) if add_step and step else value


def wanted_keep(value, low, high, plane, step_z):
    if step_z == 0:
        return 1.0 - value
    lanes = lanes_like(value)
    if step_z < 0:
        beside = rolled(low(), -Z_UP[plane])
        value = jnp.where(lanes < -step_z, beside, rolled(value, -step_z))
    else:
        beside = rolled(high(), LANES - step_z - Z_DOWN[plane])
        value = jnp.where(lanes >= LANES - step_z, beside, rolled(value, -step_z))
    return 1.0 - value


def fill_outer(extent, count, edges, fields, x_low, x_high, shifts, besides):
    size_x, size_y, _ = extent
    height = shifts.shape[3]
    at = x_place(count, REACH, size_y)
    sides = ((x_low, size_x - REACH, -LANES // 2), (x_high, 0, LANES // 2))
    for side, (source, first, high_lanes) in enumerate(sides):
        pack = kept(edges[4 + side], source[at : at + height])
        for layer in range(REACH):
            for order, field in enumerate(fields):
                lane_of = (first + layer) * SLOT + field * REACH
                besides[order, side * REACH + layer] = beside_columns(
                    pack, pack, lane_of, high_lanes
                )
    for side, (source, _, _) in enumerate(sides):
        for layer in range(REACH):
            distance = REACH - layer if side == 0 else layer + 1
            low, high = x_span(distance, size_y)
            for order, field in enumerate(fields):
                start = x_place(field, distance, size_y)
                for step, value in each_shift(
                    kept(edges[4 + side], source[start : start + high - low]),
                    besides[order, side * REACH + layer, low:high],
                    field == 2, reach_beside(distance),
                ):
                    shifts[step, order, side * REACH + layer, low:high] = value


def weights_early_kernel(
    extent, edges, broken_in, stiffness, z_low, z_high, weights, keeps,
    shifts, planes, besides, broken, sems,
):
    size_x, size_y, _ = extent

    def layer_copy(layer):
        return pltpu.make_async_copy(broken_in.at[:, layer], broken.at[:, layer], sems.at[layer])

    for layer in range(size_x):
        layer_copy(layer).start()
    low_pack = kept(edges[0], z_low[0:size_y])
    high_pack = kept(edges[1], z_high[0:size_y])
    for layer in range(size_x):
        besides[layer] = beside_columns(low_pack, high_pack, layer * SLOT + 3 * REACH)
    for layer in range(size_x):
        for order, value in each_shift(stiffness[layer], besides[layer], False):
            shifts[order, layer, FIRST : FIRST + size_y] = value

    def fill(layer, carry):
        layer_copy(layer).wait()
        for plane in range(len(OFFSETS)):
            planes[plane, layer, FIRST : FIRST + size_y] = broken[plane, layer].astype(jnp.float32)
        return carry

    lax.fori_loop(0, size_x, fill, 0)
    for late, target in ((False, weights), (True, keeps)):
        for step, first, last, bonds, base in inner_plan(extent, late)[0]:

            def one_layer(layer, carry, step=step, first=first, bonds=bonds, base=base):
                slot = base + (layer - first) * len(bonds)
                far_layer = layer + step
                for order, (tile, step_y, step_z, plane, owner) in enumerate(bonds):
                    rows = slice(8 * tile, 8 * tile + 8)
                    far_rows = slice(FIRST + step_y + 8 * tile, FIRST + step_y + 8 * tile + 8)
                    if owner:
                        keep = 1.0 - broken[plane, layer, rows].astype(jnp.float32)
                    else:
                        at = size_y + far_layer * size_y + step_y + 8 * tile
                        keep = wanted_keep(
                            planes[plane, far_layer, far_rows],
                            lambda: z_low[pl.ds(at, 8)],
                            lambda: z_high[pl.ds(at, 8)],
                            plane, step_z,
                        )
                    keep = (0.5 * C_BOND) * keep
                    if not late:
                        far = shifts[step_z + REACH, far_layer, far_rows]
                        keep = jnp.where(far > 0.0, keep * (stiffness[layer, rows] + far), 0.0)
                    target[slot + order] = keep
                return carry

            lax.fori_loop(first, last, one_layer, 0)


def weights_late_kernel(
    extent, stiffness, wide, wide_pack, wide_broken, rows_low, rows_high, keeps, weights,
    shifts, besides,
):
    size_x, size_y, _ = extent
    for layer in range(size_x):
        besides[layer] = beside_columns(wide_pack[0], wide_pack[1], layer * SLOT + 3 * REACH)
    for layer in range(size_x):
        for order, value in each_shift(wide[0, layer], besides[layer], False):
            shifts[order, layer] = value
    for step, first, last, bonds, base in inner_plan(extent, True)[0]:

        def one_layer(layer, carry, step=step, first=first, bonds=bonds, base=base):
            slot = base + (layer - first) * len(bonds)
            far_layer = layer + step
            sublanes = lax.broadcasted_iota(jnp.int32, (8, LANES), 0)
            for order, (tile, step_y, step_z, plane, owner) in enumerate(bonds):
                rows = slice(8 * tile, 8 * tile + 8)
                far_rows = slice(REACH + step_y + 8 * tile, REACH + step_y + 8 * tile + 8)
                keep = keeps[slot + order]
                if not owner:
                    if step_y < 0:
                        at = PAD + Y_UP[plane] * size_x - far_layer * step_y
                        value = rows_low[pl.ds(at, 8)]
                        across = sublanes < -step_y
                    else:
                        at = PAD + Y_DOWN[plane] * size_x + far_layer * step_y + step_y - 8
                        value = rows_high[pl.ds(at, 8)]
                        across = sublanes >= 8 - step_y
                    halo = wanted_keep(
                        value,
                        lambda: wide_broken[0, far_layer, far_rows],
                        lambda: wide_broken[1, far_layer, far_rows],
                        plane, step_z,
                    )
                    keep = jnp.where(across, (0.5 * C_BOND) * halo, keep)
                far = shifts[step_z + REACH, far_layer, far_rows]
                weights[slot + order] = jnp.where(
                    far > 0.0, keep * (stiffness[layer, rows] + far), 0.0
                )
            return carry

        lax.fori_loop(first, last, one_layer, 0)


def weights_outer_kernel(
    extent, edges, stiffness, pore, wide, wide_pack, x_up, x_broken, x_low, x_high,
    weights, pressing, shifts, planes, besides,
):
    size_x, size_y, _ = extent
    height = wide.shape[2]
    pore_at = x_place(4, REACH, size_y) + height
    broken_at = pore_at + size_y
    rows_at = broken_at + 2 * NEAR * height
    fill_outer(extent, 4, edges, (3,), x_low, x_high, shifts, besides)
    for plane, (a, b, _) in enumerate(OFFSETS):
        for layer in range(a):
            at = (X_UP[plane] + layer) * size_y
            place = X_UP[plane] + layer
            planes[place, REACH : REACH + size_y] = x_broken[at : at + size_y]
            at = rows_at + XY_UP.get(plane, 0) + layer * abs(b)
            if b > 0:
                planes[place, REACH - b : REACH] = x_low[at : at + b]
            if b < 0:
                planes[place, REACH + size_y : REACH + size_y - b] = x_low[at : at - b]
    for step, first, last, bonds, base in outer_plan(extent)[0]:
        for layer in range(first, last):
            slot = base + (layer - first) * len(bonds)
            far_layer = layer + step
            far_layer = far_layer + REACH if far_layer < 0 else far_layer - size_x + REACH
            for order, (tile, step_y, step_z, plane, owner) in enumerate(bonds):
                rows = slice(8 * tile, 8 * tile + 8)
                far_rows = slice(REACH + step_y + 8 * tile, REACH + step_y + 8 * tile + 8)
                far = shifts[step_z + REACH, 0, far_layer, far_rows]
                if owner:
                    at = (X_UP[plane] + layer - first) * size_y + 8 * tile
                    keep = 1.0 - x_up[at : at + 8]
                else:
                    low_at = broken_at + (far_layer + NEAR - REACH) * height
                    high_at = low_at + NEAR * height
                    keep = wanted_keep(
                        planes[X_UP[plane] + layer, far_rows],
                        lambda: x_low[far_rows.start + low_at : far_rows.stop + low_at],
                        lambda: x_low[far_rows.start + high_at : far_rows.stop + high_at],
                        plane, step_z,
                    )
                value = keep * (0.5 * C_BOND) * (stiffness[layer, rows] + far)
                weights[slot + order] = jnp.where(far > 0.0, value, 0.0)

    middle = slice(REACH, REACH + size_y)

    def wide_field(field, layer):
        if layer < 0 or layer >= size_x:
            source = x_low if layer < 0 else x_high
            at = x_place(field, 1, size_y) + reach_beside(1) if field == 3 else pore_at
            return kept(edges[4 if layer < 0 else 5], source[at : at + size_y])
        return wide[field - 3, layer, middle]

    for layer in range(size_x):
        own = pore[layer]
        for axis in range(3):
            total = jnp.zeros((size_y, LANES), jnp.float32)
            for sign in (1, -1):
                if axis == 0:
                    inside = wide_field(3, layer + sign)
                    level = wide_field(4, layer + sign)
                elif axis == 1:
                    rows = slice(REACH + sign, REACH + sign + size_y)
                    inside = wide[0, layer, rows]
                    level = wide[1, layer, rows]
                else:
                    inside, level = (
                        moved(
                            wide[field - 3, layer],
                            beside_columns(
                                wide_pack[0], wide_pack[1], layer * SLOT + field * REACH
                            ),
                            sign,
                        )[middle]
                        for field in (3, 4)
                    )
                total = total + jnp.where(inside > 0.0, (-0.5 * sign) * (level - own), 0.0)
            pressing[axis, layer] = total


def add_bonds(bonds, step, layer, far_layer, first_row, motion, shifts, weights, slot, total):
    for tile in sorted({bond[0] for bond in bonds}):
        rows = slice(8 * tile, 8 * tile + 8)
        own = [motion[axis, layer, rows] for axis in range(3)]
        near_x = own[0] - float(step)
        near_y = {step_y: own[1] - float(step_y) for step_y in range(-REACH, REACH + 1)}
        force = [total[axis, layer, rows] for axis in range(3)]
        for order, (bond_tile, step_y, step_z, plane, _) in enumerate(bonds):
            if bond_tile != tile:
                continue
            far_rows = slice(first_row + step_y + 8 * tile, first_row + step_y + 8 * tile + 8)
            far = [shifts[step_z + REACH, axis, far_layer, far_rows] for axis in range(3)]
            radial = [far[0] - near_x, far[1] - near_y[step_y], far[2] - own[2]]
            square = radial[0] * radial[0] + radial[1] * radial[1] + radial[2] * radial[2]
            rest = math.sqrt(sum(part * part for part in OFFSETS[plane]))
            factor = weights[slot + order] * (1.0 / rest - lax.rsqrt(square))
            force = [force[axis] + factor * radial[axis] for axis in range(3)]
        for axis in range(3):
            total[axis, layer, rows] = force[axis]


def add_inner(extent, late, fill, motion, shifts, weights, total):
    lax.fori_loop(0, extent[0], fill, 0, unroll=UNROLL_FILL)
    for step, first, last, bonds, base in inner_plan(extent, late)[0]:
        if not bonds:
            continue

        def one_layer(layer, carry, step=step, first=first, bonds=bonds, base=base):
            slot = base + (layer - first) * len(bonds)
            add_bonds(bonds, step, layer, layer + step, FIRST, motion, shifts, weights, slot, total)
            return carry

        lax.fori_loop(first, last, one_layer, 0, unroll=UNROLL if last - first > 1 else 1)


def force_early_kernel(extent, edges, motion, z_low, z_high, weights, total, shifts, besides):
    size_x, size_y, _ = extent
    total[...] = jnp.zeros(total.shape, jnp.float32)
    low_pack = kept(edges[0], z_low[0:size_y])
    high_pack = kept(edges[1], z_high[0:size_y])
    for layer in range(size_x):
        for axis in range(3):
            besides[axis, layer] = beside_columns(
                low_pack, high_pack, layer * SLOT + axis * REACH
            )

    def fill(layer, carry):
        for axis in range(3):
            for order, value in each_shift(motion[axis, layer], besides[axis, layer], axis == 2):
                shifts[order, axis, layer, FIRST : FIRST + size_y] = value
        return carry

    add_inner(extent, False, fill, motion, shifts, weights, total)


def force_late_kernel(
    extent, count, edges, motion, early, early_shifts, y_low, y_high, weights,
    total, shifts, halo, besides,
):
    size_x, size_y, _ = extent
    total[...] = early[...]
    middle = slice(FIRST, FIRST + size_y)
    above = FIRST + size_y

    def across(place, at):
        halo[place, 0:REACH] = kept(edges[3], y_high[at : at + REACH])
        halo[place, REACH : 8 - REACH] = jnp.zeros((8 - 2 * REACH, LANES), jnp.float32)
        halo[place, 8 - REACH : 8] = kept(edges[2], y_low[at : at + REACH])

    packs = 3 * size_x
    for order in range(2):
        across(packs + order, (count * size_x + order) * REACH)
    for place in range(3 * size_x):
        across(place, place * REACH)
    low_pack, high_pack = halo[packs], halo[packs + 1]
    for layer in range(size_x):
        for axis in range(3):
            besides[axis * size_x + layer] = beside_columns(
                low_pack, high_pack, layer * SLOT + axis * REACH
            )

    def fill(layer, carry):
        for axis in range(3):
            place = axis * size_x + layer
            for order, value in each_shift(halo[place], besides[place], axis == 2):
                shifts[order, axis, layer, middle] = early_shifts[order, axis, layer, middle]
                shifts[order, axis, layer, FIRST - REACH : FIRST] = value[8 - REACH : 8]
                shifts[order, axis, layer, above : above + REACH] = value[0:REACH]
        return carry

    add_inner(extent, True, fill, motion, shifts, weights, total)


def finish_kernel(
    extent, count, stage, edges, motion, speed, pressing, inner, weights, x_low, x_high, *refs
):
    size_x, size_y, _ = extent
    if stage == "last":
        motion_out, speed_out, accel_out, total, shifts, besides = refs
    else:
        motion_out, speed_out, z_up, z_down, total, shifts, besides = refs
    total[...] = inner[...] + pressing[...]
    fill_outer(extent, count, edges, range(3), x_low, x_high, shifts, besides)
    for step, first, last, bonds, base in outer_plan(extent)[0]:
        for layer in range(first, last):
            slot = base + (layer - first) * len(bonds)
            far_layer = layer + step + (REACH if step < 0 else REACH - size_x)
            add_bonds(bonds, step, layer, far_layer, REACH, motion, shifts, weights, slot, total)
    accel = total[...]
    new_speed = speed[...] + HALF_DT * accel
    if stage == "last":
        motion_out[...] = motion[...]
        speed_out[...] = new_speed
        accel_out[...] = accel
        return
    if stage == "middle":
        new_speed = new_speed + HALF_DT * accel
    speed_out[...] = new_speed
    motion_out[...] = motion[...] + DT_STEP * new_speed
    up, down = pack_columns(lambda axis, layer: motion_out[axis, layer], 3, size_x, size_y)
    z_up[...] = up
    z_down[...] = down


VMEM = pl.BlockSpec(memory_space=pltpu.VMEM)
SMEM = pl.BlockSpec(memory_space=pltpu.SMEM)


def call(kernel, scalars, operands, shapes, scratch=(), name=None, results=(), far=()):
    operands = [pltpu.with_memory_space_constraint(operand, pltpu.HBM) for operand in far] + [
        pltpu.with_memory_space_constraint(operand, pltpu.VMEM) for operand in operands
    ]
    return pl.pallas_call(
        kernel,
        out_shape=[
            jax.ShapeDtypeStruct(shape, jnp.float32)
            if place in results
            else pltpu.VMEM(shape, jnp.float32)
            for place, shape in enumerate(shapes)
        ],
        in_specs=[SMEM] * len(scalars)
        + [pl.BlockSpec(memory_space=pltpu.HBM)] * len(far)
        + [VMEM] * (len(operands) - len(far)),
        out_specs=[VMEM] * len(shapes),
        scratch_shapes=[
            pltpu.VMEM(item, jnp.float32) if isinstance(item, tuple) else item for item in scratch
        ],
        compiler_params=pltpu.CompilerParams(vmem_limit_bytes=24 * 1024 * 1024),
        name=name,
    )(*scalars, *operands)


def sent(value, axis, distance):
    count = lax.axis_size(axis)
    return lax.ppermute(value, axis, [(i, (i + distance) % count) for i in range(count)])


def on_device(displacement, velocity, stiffness, broken, borehole_id, flags, pressure):
    extent = stiffness.shape
    size_x, size_y, _ = extent
    height = size_y + 8
    tall = size_y + 2 * FIRST
    edges = jnp.stack(
        [
            end
            for axis in ("gz", "gy", "gx")
            for end in (
                (lax.axis_index(axis) > 0).astype(jnp.int32),
                (lax.axis_index(axis) < lax.axis_size(axis) - 1).astype(jnp.int32),
            )
        ]
    )
    field = (size_x, size_y, LANES)
    vector = (3,) + field
    part = functools.partial

    pack = (size_y + size_x * size_y + PAD, LANES)
    rows_shapes = [(count * size_x + 2 * PAD, LANES) for count in (Y_UP_COUNT, Y_DOWN_COUNT)]
    layers_shape = (X_UP_COUNT * size_y, LANES)
    motion, stiffness, pore, z_up, z_down, rows_up, rows_down, x_up = pl.pallas_call(
        part(start_kernel, extent),
        out_shape=[
            pltpu.VMEM(shape, kind)
            for shape, kind in (
                (vector, jnp.float32), (field, jnp.float32),
                (field, jnp.float32), (pack, jnp.float32), (pack, jnp.float32),
                (rows_shapes[0], jnp.float32), (rows_shapes[1], jnp.float32),
                (layers_shape, jnp.float32),
            )
        ],
        in_specs=[pl.BlockSpec(memory_space=pltpu.HBM)] * 6,
        out_specs=[VMEM] * 8,
        scratch_shapes=[
            pltpu.VMEM(broken.shape, jnp.int32),
            pltpu.SMEM(pressure.shape, jnp.float32),
            pltpu.VMEM(field, jnp.int32),
            pltpu.VMEM(field, jnp.int32),
            pltpu.SemaphoreType.DMA((5,)),
            pltpu.SemaphoreType.DMA((size_x,)),
        ],
        compiler_params=pltpu.CompilerParams(vmem_limit_bytes=24 * 1024 * 1024),
        name="start",
    )(
        *(
            pltpu.with_memory_space_constraint(operand, pltpu.HBM)
            for operand in (pressure, displacement, stiffness, borehole_id, flags, broken)
        )
    )
    z_low = sent(z_up, "gz", 1)
    z_high = sent(z_down, "gz", -1)
    rows_low = sent(rows_up, "gy", 1)
    rows_high = sent(rows_down, "gy", -1)
    x_broken = sent(x_up, "gx", 1)
    rows = (round_up(5 * size_x * REACH + 2 * REACH + 2 * size_x * REACH), LANES)
    y_up, y_down = call(
        part(y_rows_first_kernel, extent), [edges],
        [motion, stiffness, pore, z_low, z_high], [rows, rows], name="y_rows_first",
    )
    y_low = sent(y_up, "gy", 1)
    y_high = sent(y_down, "gy", -1)
    moves = 2 * REACH + 1
    early_slots = inner_plan(extent, False)[1]
    late_slots = inner_plan(extent, True)[1]
    outer_slots = outer_plan(extent)[1]
    weights_early, keeps = call(
        part(weights_early_kernel, extent), [edges], [stiffness, z_low, z_high],
        [(early_slots, 8, LANES), (late_slots, 8, LANES)],
        [
            (moves, size_x, tall, LANES),
            (len(OFFSETS), size_x, tall, LANES),
            field,
            pltpu.VMEM(broken.shape, jnp.int32),
            pltpu.SemaphoreType.DMA((size_x,)),
        ], name="weights_early", far=[broken],
    )

    def force_early(motion, z_low, z_high):
        return call(
            part(force_early_kernel, extent), [edges], [motion, z_low, z_high, weights_early],
            [vector, (moves, 3, size_x, tall, LANES)], [vector], name="force_early",
        )

    def force_late(count, motion, early, early_shifts, y_low, y_high):
        return call(
            part(force_late_kernel, extent, count), [edges],
            [motion, early, early_shifts, y_low, y_high, weights_late], [vector],
            [(moves, 3, size_x, tall, LANES), (2 + 3 * size_x, 8, LANES), (3 * size_x, 8, LANES)], name="force_late",
        )[0]

    early, early_shifts = force_early(motion, z_low, z_high)
    y_low, y_high, x_broken, early = lax.optimization_barrier((y_low, y_high, x_broken, early))
    layers = x_place(4, REACH, size_y) + height + size_y
    wide_static, wide_pack, wide_broken, x_fields_up, x_fields_down = call(
        part(x_layers_first_kernel, extent), [edges],
        [motion, stiffness, pore, z_low, z_high, y_low, y_high, rows_low, rows_high],
        [
            (2, size_x, height, LANES),
            (2, height, LANES),
            (2, size_x, height, LANES),
            (round_up(layers + 2 * NEAR * height + XY_UP_COUNT), LANES),
            (round_up(layers), LANES),
        ], [(3, size_x, height, LANES)], name="x_layers_first",
    )
    x_low = sent(x_fields_up, "gx", 1)
    x_high = sent(x_fields_down, "gx", -1)
    (weights_late,) = call(
        part(weights_late_kernel, extent), [],
        [stiffness, wide_static, wide_pack, wide_broken, rows_low, rows_high, keeps],
        [(late_slots, 8, LANES)],
        [(moves, size_x, height, LANES), (size_x, height, LANES)], name="weights_late",
    )
    inner = force_late(5, motion, early, early_shifts, y_low, y_high)
    outer_weights, pressing = call(
        part(weights_outer_kernel, extent), [edges],
        [stiffness, pore, wide_static, wide_pack, x_up, x_broken, x_low, x_high],
        [(outer_slots, 8, LANES), vector],
        [
            (moves, 1, 2 * REACH, height, LANES),
            (X_UP_COUNT, height, LANES),
            (1, 2 * REACH, height, LANES),
        ], name="weights_outer",
    )

    def finish(stage, count, motion, speed, inner, x_low, x_high):
        columns = (size_y, LANES)
        shapes = [vector] * 3 if stage == "last" else [vector, vector, columns, columns]
        return call(
            part(finish_kernel, extent, count, stage), [edges],
            [motion, speed, pressing, inner, outer_weights, x_low, x_high],
            shapes,
            [
                vector,
                (moves, 3, 2 * REACH, height, LANES),
                (3, 2 * REACH, height, LANES),
            ], name="finish_" + stage,
            results=(0, 1, 2) if stage == "last" else (),
        )

    motion, speed, z_up, z_down = finish(
        "first", 4, motion, velocity, inner, x_low, x_high
    )
    for step_index in range(STEPS):
        z_low = sent(z_up, "gz", 1)
        z_high = sent(z_down, "gz", -1)
        rows = (round_up(3 * size_x * REACH + 2 * REACH), LANES)
        y_up, y_down = call(
            part(y_rows_kernel, extent), [edges], [motion, z_low, z_high], [rows, rows],
            name="y_rows",
        )
        y_low = sent(y_up, "gy", 1)
        y_high = sent(y_down, "gy", -1)
        early, early_shifts = force_early(motion, z_low, z_high)
        y_low, y_high, early = lax.optimization_barrier((y_low, y_high, early))
        layers = round_up(x_place(3, REACH, size_y) + height)
        x_up, x_down = call(
            part(x_layers_kernel, extent), [edges],
            [motion, z_low, z_high, y_low, y_high],
            [(layers, LANES), (layers, LANES)],
            [(3, size_x, height, LANES), (2, height, LANES)], name="x_layers",
        )
        x_low = sent(x_up, "gx", 1)
        x_high = sent(x_down, "gx", -1)
        inner = force_late(3, motion, early, early_shifts, y_low, y_high)
        if step_index < STEPS - 1:
            motion, speed, z_up, z_down = finish("middle", 3, motion, speed, inner, x_low, x_high)
        else:
            motion, speed, accel = finish("last", 3, motion, speed, inner, x_low, x_high)
    return (motion, speed, accel)


def solution(mesh):
    in_specs = (
        P(None, "gx", "gy", "gz"),
        P(None, "gx", "gy", "gz"),
        P("gx", "gy", "gz"),
        P(None, "gx", "gy", "gz"),
        P("gx", "gy", "gz"),
        P("gx", "gy", "gz"),
        P(),
    )
    out_specs = (P(None, "gx", "gy", "gz"), P(None, "gx", "gy", "gz"), P(None, "gx", "gy", "gz"))
    return jax.shard_map(
        on_device, mesh=mesh, in_specs=in_specs, out_specs=out_specs, check_vma=False
    )
```

profile of v0, /device:TPU:71, one launch (start us, length us, event | category | flops | bytes accessed | tf_op | source)
XLA Modules:
  0.0 94.5 jit_solution(12313811014880890833)
XLA Ops:
  0.6 3.9 %start.1 = (f32[3,8,16,128]{3,2,1,0:T(8,128)S(1)}, f32[8,16,128]{2,1,0:T(8,128)S(1)}, f32[8,16,128]{2,1,0:T(8,128)S(1)}, f32[152,128]{1,0:T(8,128)S(1)}, f32[152...) custom-call(f32[8]{0:T(128)} %pressure_in.1, ...), custom_call_target="tpu_custom_call" | custom-call | tf_op jit(solution)/shard_map/start/pallas_call | solution.py:793
  4.5 4.8 %collective-permute-start.4 = (f32[1120,128]{1,0:T(8,128)S(1)}, f32[1120,128]{1,0:T(8,128)S(1)}, u32[]{:S(2)}, u32[]{:S(2)}) collective-permute-start(f32[1120,128]{1,0:T(8,128)S(1)} %get-tuple-element.61.x_up), channel_id=1, source_target_pairs={{0,32},{32,64},{64,96},{96,128},{128,160},{160,192},{192,224},{224... | collective-permute-start | bytes 1720328 | tf_op jit(solution)/shard_map/ppermute | solution.py:768
  10.3 1.3 %collective-permute-start.1 = (f32[152,128]{1,0:T(8,128)S(1)}, f32[152,128]{1,0:T(8,128)S(1)}, u32[]{:S(2)}, u32[]{:S(2)}) collective-permute-start(f32[152,128]{1,0:T(8,128)S(1)} %get-tuple-element.58), channel_id=1, source_target_pairs={{0,3},{1,0},{2,1},{3,2},{4,7},{5,4},{6,5},{7,6},{8,11},{9,8},{10,9... | collective-permute-start | bytes 233480 | tf_op jit(solution)/shard_map/ppermute | solution.py:768
  11.5 2.8 %collective-permute-start.6 = (f32[224,128]{1,0:T(8,128)S(1)}, f32[224,128]{1,0:T(8,128)S(1)}, u32[]{:S(2)}, u32[]{:S(2)}) collective-permute-start(f32[224,128]{1,0:T(8,128)S(1)} %get-tuple-element.67), channel_id=1, source_target_pairs={{0,28},{4,0},{8,4},{12,8},{16,12},{20,16},{24,20},{28,24},{1,29},{... | collective-permute-start | bytes 344072 | tf_op jit(solution)/shard_map/ppermute | solution.py:768
  15.5 1.8 %collective-permute-start.2 = (f32[176,128]{1,0:T(8,128)S(1)}, f32[176,128]{1,0:T(8,128)S(1)}, u32[]{:S(2)}, u32[]{:S(2)}) collective-permute-start(f32[176,128]{1,0:T(8,128)S(1)} %get-tuple-element.59), channel_id=1, source_target_pairs={{0,4},{4,8},{8,12},{12,16},{16,20},{20,24},{24,28},{28,0},{1,5},{5... | collective-permute-start | bytes 270344 | tf_op jit(solution)/shard_map/ppermute | solution.py:768
  17.3 1.8 %collective-permute-start.3 = (f32[176,128]{1,0:T(8,128)S(1)}, f32[176,128]{1,0:T(8,128)S(1)}, u32[]{:S(2)}, u32[]{:S(2)}) collective-permute-start(f32[176,128]{1,0:T(8,128)S(1)} %get-tuple-element.60), channel_id=1, source_target_pairs={{0,28},{4,0},{8,4},{12,8},{16,12},{20,16},{24,20},{28,24},{1,29},{... | collective-permute-start | bytes 270344 | tf_op jit(solution)/shard_map/ppermute | solution.py:768
  19.1 7.9 %weights_early.1 = (f32[1024,8,128]{2,1,0:T(8,128)S(1)}, f32[648,8,128]{2,1,0:T(8,128)S(1)}) custom-call(s32[6]{0:T(128)S(1)} %stack.36.edges, s32[61,8,16,128]{3,2,1,0:T(8,128)} %broken_in.3, f32[8,16,128]{2,1,0:T(8,128)S(1)} %get-tuple-element.55.stiffness, f32[152,128]{1,0:T(8,128)S(1)} %collective-permute-done.z_low, ...), custom_call_target="tpu_custom_call" | custom-call | tf_op jit(solution)/shard_map/weights_early/pallas_call | solution.py:746
  27.0 4.0 %force_early.3 = (f32[3,8,16,128]{3,2,1,0:T(8,128)S(1)}, f32[7,3,8,32,128]{4,3,2,1,0:T(8,128)S(1)}) custom-call(s32[6]{0:T(128)S(1)} %stack.36.edges, f32[3,8,16,128]{3,2,1,0:T(8,128)S(1)} %get-tuple-element.54.motion, f32[152,128]{1,0:T(8,128)S(1)} %collective-permute-done.z_low, f32[152,128]{1,0:T(8,128)S(1)} %collective-permute-done.1.z_high, ...), custom_call_target="tpu_custom_call" | custom-call | tf_op jit(solution)/shard_map/force_early/pallas_call | solution.py:746
  31.8 3.1 %collective-permute-start.7 = (f32[440,128]{1,0:T(8,128)S(1)}, f32[440,128]{1,0:T(8,128)S(1)}, u32[]{:S(2)}, u32[]{:S(2)}) collective-permute-start(f32[440,128]{1,0:T(8,128)S(1)} %get-tuple-element.71), channel_id=1, source_target_pairs={{0,32},{32,64},{64,96},{96,128},{128,160},{160,192},{192,224},{224... | collective-permute-start | bytes 675848 | tf_op jit(solution)/shard_map/ppermute | solution.py:768
  34.9 2.6 %weights_late.1.weights = f32[648,8,128]{2,1,0:T(8,128)S(1)} custom-call(f32[8,16,128]{2,1,0:T(8,128)S(1)} %get-tuple-element.55.stiffness, f32[2,8,24,128]{3,2,1,0:T(8,128)S(1)} %get-tuple-element.68.wide, f32[2,24,128]{2,1,0:T(8,128)S(1)} %get-tuple-element.69.wide_pack, f32[2,8,24,128]{3,2,1,0:T(8,128)S(1)} %get-tuple-element.76.wide_broken, ...), custom_call_target="tpu_custom_call" | custom-call | tf_op jit(solution)/shard_map/weights_late/pallas_call | solution.py:746
  37.5 2.9 %force_late.3.inner = f32[3,8,16,128]{3,2,1,0:T(8,128)S(1)} custom-call(s32[6]{0:T(128)S(1)} %stack.36.edges, f32[3,8,16,128]{3,2,1,0:T(8,128)S(1)} %get-tuple-element.54.motion, f32[3,8,16,128]{3,2,1,0:T(8,128)S(1)} %get-tuple-element.74.early, f32[7,3,8,32,128]{4,3,2,1,0:T(8,128)S(1)} %get-tuple-element.75.early_shifts, ...), custom_call_target="tpu_custom_call" | custom-call | tf_op jit(solution)/shard_map/force_late/pallas_call | solution.py:746
  40.5 2.3 %collective-permute-done.8.x_high = f32[264,128]{1,0:T(8,128)S(1)} collective-permute-done((f32[264,128]{1,0:T(8,128)S(1)}, f32[264,128]{1,0:T(8,128)S(1)}, u32[]{:S(2)}, u32[]{:S(2)}) %collective-permute-start.8) | collective-permute-done | bytes 135200 | tf_op jit(solution)/shard_map/ppermute | solution.py:768
  42.8 1.9 %weights_outer.1 = (f32[280,8,128]{2,1,0:T(8,128)S(1)}, f32[3,8,16,128]{3,2,1,0:T(8,128)S(1)}) custom-call(s32[6]{0:T(128)S(1)} %stack.36.edges, f32[8,16,128]{2,1,0:T(8,128)S(1)} %get-tuple-element.55.stiffness, f32[8,16,128]{2,1,0:T(8,128)S(1)} %get-tuple-element.56.pore, f32[2,8,24,128]{3,2,1,0:T(8,128)S(1)} %get-tuple-element.68.wide, ...), custom_call_target="tpu_custom_call" | custom-call | tf_op jit(solution)/shard_map/weights_outer/pallas_call | solution.py:746
  44.7 1.7 %finish_first.1 = (f32[3,8,16,128]{3,2,1,0:T(8,128)S(1)}, f32[3,8,16,128]{3,2,1,0:T(8,128)S(1)}, f32[16,128]{1,0:T(8,128)S(1)}, f32[16,128]{1,0:T(8,128)S(1)}) custom-call(s32[6]{0:T(128)S(1)} %stack.36.edges, f32[3,8,16,128]{3,2,1,0:T(8,128)S(1)} %get-tuple-element.54.motion, f32[3,8,16,128]{3,2,1,0:T(8,128)S(1)} %copy-done, ...), custom_call_target="tpu_custom_call" | custom-call | tf_op jit(solution)/shard_map/finish_first/pallas_call | solution.py:746
  46.5 1.4 %collective-permute-start.10 = (f32[16,128]{1,0:T(8,128)S(1)}, f32[16,128]{1,0:T(8,128)S(1)}, u32[]{:S(2)}, u32[]{:S(2)}) collective-permute-start(f32[16,128]{1,0:T(8,128)S(1)} %get-tuple-element.82), channel_id=1, source_target_pairs={{0,3},{1,0},{2,1},{3,2},{4,7},{5,4},{6,5},{7,6},{8,11},{9,8},{10,9... | collective-permute-start | bytes 24584 | tf_op jit(solution)/shard_map/ppermute | solution.py:768
  48.0 1.0 %collective-permute-done.9.z_low = f32[16,128]{1,0:T(8,128)S(1)} collective-permute-done((f32[16,128]{1,0:T(8,128)S(1)}, f32[16,128]{1,0:T(8,128)S(1)}, u32[]{:S(2)}, u32[]{:S(2)}) %collective-permute-start.9) | collective-permute-done | bytes 8224 | tf_op jit(solution)/shard_map/ppermute | solution.py:768
  49.0 1.3 %collective-permute-done.10.z_high = f32[16,128]{1,0:T(8,128)S(1)} collective-permute-done((f32[16,128]{1,0:T(8,128)S(1)}, f32[16,128]{1,0:T(8,128)S(1)}, u32[]{:S(2)}, u32[]{:S(2)}) %collective-permute-start.10) | collective-permute-done | bytes 8224 | tf_op jit(solution)/shard_map/ppermute | solution.py:768
  51.0 3.6 %collective-permute-start.12 = (f32[80,128]{1,0:T(8,128)S(1)}, f32[80,128]{1,0:T(8,128)S(1)}, u32[]{:S(2)}, u32[]{:S(2)}) collective-permute-start(f32[80,128]{1,0:T(8,128)S(1)} %get-tuple-element.84), channel_id=1, source_target_pairs={{0,28},{4,0},{8,4},{12,8},{16,12},{20,16},{24,20},{28,24},{1,29},{... | collective-permute-start | bytes 122888 | tf_op jit(solution)/shard_map/ppermute | solution.py:768
  54.5 4.0 %force_early.4 = (f32[3,8,16,128]{3,2,1,0:T(8,128)S(1)}, f32[7,3,8,32,128]{4,3,2,1,0:T(8,128)S(1)}) custom-call(s32[6]{0:T(128)S(1)} %stack.36.edges, f32[3,8,16,128]{3,2,1,0:T(8,128)S(1)} %get-tuple-element.79.motion, f32[16,128]{1,0:T(8,128)S(1)} %collective-permute-done.9.z_low, f32[16,128]{1,0:T(8,128)S(1)} %collective-permute-done.10.z_high, ...), custom_call_target="tpu_custom_call" | custom-call | tf_op jit(solution)/shard_map/force_early/pallas_call | solution.py:746
  59.1 3.5 %collective-permute-start.13 = (f32[192,128]{1,0:T(8,128)S(1)}, f32[192,128]{1,0:T(8,128)S(1)}, u32[]{:S(2)}, u32[]{:S(2)}) collective-permute-start(f32[192,128]{1,0:T(8,128)S(1)} %get-tuple-element.90), channel_id=1, source_target_pairs={{0,32},{32,64},{64,96},{96,128},{128,160},{160,192},{192,224},{224... | collective-permute-start | bytes 294920 | tf_op jit(solution)/shard_map/ppermute | solution.py:768
  62.6 2.9 %force_late.4.inner = f32[3,8,16,128]{3,2,1,0:T(8,128)S(1)} custom-call(s32[6]{0:T(128)S(1)} %stack.36.edges, f32[3,8,16,128]{3,2,1,0:T(8,128)S(1)} %get-tuple-element.79.motion, f32[3,8,16,128]{3,2,1,0:T(8,128)S(1)} %get-tuple-element.86.early, f32[7,3,8,32,128]{4,3,2,1,0:T(8,128)S(1)} %get-tuple-element.87.early_shifts, ...), custom_call_target="tpu_custom_call" | custom-call | tf_op jit(solution)/shard_map/force_late/pallas_call | solution.py:746
  65.5 3.6 %collective-permute-done.14.x_high = f32[192,128]{1,0:T(8,128)S(1)} collective-permute-done((f32[192,128]{1,0:T(8,128)S(1)}, f32[192,128]{1,0:T(8,128)S(1)}, u32[]{:S(2)}, u32[]{:S(2)}) %collective-permute-start.14) | collective-permute-done | bytes 98336 | tf_op jit(solution)/shard_map/ppermute | solution.py:768
  69.2 1.7 %finish_middle.1 = (f32[3,8,16,128]{3,2,1,0:T(8,128)S(1)}, f32[3,8,16,128]{3,2,1,0:T(8,128)S(1)}, f32[16,128]{1,0:T(8,128)S(1)}, f32[16,128]{1,0:T(8,128)S(1)}) custom-call(s32[6]{0:T(128)S(1)} %stack.36.edges, f32[3,8,16,128]{3,2,1,0:T(8,128)S(1)} %get-tuple-element.79.motion, f32[3,8,16,128]{3,2,1,0:T(8,128)S(1)} %get-tuple-element.80.speed, ...), custom_call_target="tpu_custom_call" | custom-call | tf_op jit(solution)/shard_map/finish_middle/pallas_call | solution.py:746
  71.0 1.5 %collective-permute-start.16 = (f32[16,128]{1,0:T(8,128)S(1)}, f32[16,128]{1,0:T(8,128)S(1)}, u32[]{:S(2)}, u32[]{:S(2)}) collective-permute-start(f32[16,128]{1,0:T(8,128)S(1)} %get-tuple-element.95), channel_id=1, source_target_pairs={{0,3},{1,0},{2,1},{3,2},{4,7},{5,4},{6,5},{7,6},{8,11},{9,8},{10,9... | collective-permute-start | bytes 24584 | tf_op jit(solution)/shard_map/ppermute | solution.py:768
  72.4 1.0 %collective-permute-done.15.z_low = f32[16,128]{1,0:T(8,128)S(1)} collective-permute-done((f32[16,128]{1,0:T(8,128)S(1)}, f32[16,128]{1,0:T(8,128)S(1)}, u32[]{:S(2)}, u32[]{:S(2)}) %collective-permute-start.15) | collective-permute-done | bytes 8224 | tf_op jit(solution)/shard_map/ppermute | solution.py:768
  73.5 1.3 %collective-permute-done.16.z_high = f32[16,128]{1,0:T(8,128)S(1)} collective-permute-done((f32[16,128]{1,0:T(8,128)S(1)}, f32[16,128]{1,0:T(8,128)S(1)}, u32[]{:S(2)}, u32[]{:S(2)}) %collective-permute-start.16) | collective-permute-done | bytes 8224 | tf_op jit(solution)/shard_map/ppermute | solution.py:768
  75.7 3.6 %collective-permute-start.18 = (f32[80,128]{1,0:T(8,128)S(1)}, f32[80,128]{1,0:T(8,128)S(1)}, u32[]{:S(2)}, u32[]{:S(2)}) collective-permute-start(f32[80,128]{1,0:T(8,128)S(1)} %get-tuple-element.97), channel_id=1, source_target_pairs={{0,28},{4,0},{8,4},{12,8},{16,12},{20,16},{24,20},{28,24},{1,29},{... | collective-permute-start | bytes 122888 | tf_op jit(solution)/shard_map/ppermute | solution.py:768
  79.2 4.0 %force_early.5 = (f32[3,8,16,128]{3,2,1,0:T(8,128)S(1)}, f32[7,3,8,32,128]{4,3,2,1,0:T(8,128)S(1)}) custom-call(s32[6]{0:T(128)S(1)} %stack.36.edges, f32[3,8,16,128]{3,2,1,0:T(8,128)S(1)} %get-tuple-element.92.motion, f32[16,128]{1,0:T(8,128)S(1)} %collective-permute-done.15.z_low, f32[16,128]{1,0:T(8,128)S(1)} %collective-permute-done.16.z_high, ...), custom_call_target="tpu_custom_call" | custom-call | tf_op jit(solution)/shard_map/force_early/pallas_call | solution.py:746
  83.8 2.2 %collective-permute-start.19 = (f32[192,128]{1,0:T(8,128)S(1)}, f32[192,128]{1,0:T(8,128)S(1)}, u32[]{:S(2)}, u32[]{:S(2)}) collective-permute-start(f32[192,128]{1,0:T(8,128)S(1)} %get-tuple-element.103), channel_id=1, source_target_pairs={{0,32},{32,64},{64,96},{96,128},{128,160},{160,192},{192,224},{224... | collective-permute-start | bytes 294920 | tf_op jit(solution)/shard_map/ppermute | solution.py:768
  86.0 2.9 %force_late.5.inner = f32[3,8,16,128]{3,2,1,0:T(8,128)S(1)} custom-call(s32[6]{0:T(128)S(1)} %stack.36.edges, f32[3,8,16,128]{3,2,1,0:T(8,128)S(1)} %get-tuple-element.92.motion, f32[3,8,16,128]{3,2,1,0:T(8,128)S(1)} %get-tuple-element.99.early, f32[7,3,8,32,128]{4,3,2,1,0:T(8,128)S(1)} %get-tuple-element.100.early_shifts, ...), custom_call_target="tpu_custom_call" | custom-call | tf_op jit(solution)/shard_map/force_late/pallas_call | solution.py:746
  88.9 3.2 %collective-permute-done.20.x_high = f32[192,128]{1,0:T(8,128)S(1)} collective-permute-done((f32[192,128]{1,0:T(8,128)S(1)}, f32[192,128]{1,0:T(8,128)S(1)}, u32[]{:S(2)}, u32[]{:S(2)}) %collective-permute-start.20) | collective-permute-done | bytes 98336 | tf_op jit(solution)/shard_map/ppermute | solution.py:768
  92.1 2.3 %finish_last.1 = (f32[3,8,16,128]{3,2,1,0:T(8,128)}, f32[3,8,16,128]{3,2,1,0:T(8,128)}, f32[3,8,16,128]{3,2,1,0:T(8,128)}) custom-call(s32[6]{0:T(128)S(1)} %stack.36.edges, f32[3,8,16,128]{3,2,1,0:T(8,128)S(1)} %get-tuple-element.92.motion, f32[3,8,16,128]{3,2,1,0:T(8,128)S(1)} %get-tuple-element.93.speed, ...), custom_call_target="tpu_custom_call" | custom-call | tf_op jit(solution)/shard_map/finish_last/pallas_call | solution.py:746
  (33 shorter events, 5.7 us)
Async XLA Ops:
  4.5 26.6 %collective-permute-start.4 = (f32[1120,128]{1,0:T(8,128)S(1)}, f32[1120,128]{1,0:T(8,128)S(1)}, u32[]{:S(2)}, u32[]{:S(2)}) collective-permute-start(f32[1120,128]{1,0:T(8,128)S(1)} %get-tuple-element.61.x_up), channel_id=1, source_target_pairs={{0,32},{32,64},{64,96},{96,128},{128,160},{160,192},{192,224},{224... | collective-permute-start | bytes 1720328 | tf_op jit(solution)/shard_map/ppermute | solution.py:768
  9.3 21.7 %collective-permute-start.5 = (f32[368,128]{1,0:T(8,128)S(1)}, f32[368,128]{1,0:T(8,128)S(1)}, u32[]{:S(2)}, u32[]{:S(2)}) collective-permute-start(f32[368,128]{1,0:T(8,128)S(1)} %get-tuple-element.66), channel_id=1, source_target_pairs={{0,4},{4,8},{8,12},{12,16},{16,20},{20,24},{24,28},{28,0},{1,5},{5... | collective-permute-start | bytes 565256 | tf_op jit(solution)/shard_map/ppermute | solution.py:768
  10.1 4.4 %collective-permute-start = (f32[152,128]{1,0:T(8,128)S(1)}, f32[152,128]{1,0:T(8,128)S(1)}, u32[]{:S(2)}, u32[]{:S(2)}) collective-permute-start(f32[152,128]{1,0:T(8,128)S(1)} %get-tuple-element.57), channel_id=1, source_target_pairs={{0,1},{1,2},{2,3},{3,0},{4,5},{5,6},{6,7},{7,4},{8,9},{9,10},{10,1... | collective-permute-start | bytes 233480 | tf_op jit(solution)/shard_map/ppermute | solution.py:768
  10.3 4.6 %collective-permute-start.1 = (f32[152,128]{1,0:T(8,128)S(1)}, f32[152,128]{1,0:T(8,128)S(1)}, u32[]{:S(2)}, u32[]{:S(2)}) collective-permute-start(f32[152,128]{1,0:T(8,128)S(1)} %get-tuple-element.58), channel_id=1, source_target_pairs={{0,3},{1,0},{2,1},{3,2},{4,7},{5,4},{6,5},{7,6},{8,11},{9,8},{10,9... | collective-permute-start | bytes 233480 | tf_op jit(solution)/shard_map/ppermute | solution.py:768
  11.5 19.5 %collective-permute-start.6 = (f32[224,128]{1,0:T(8,128)S(1)}, f32[224,128]{1,0:T(8,128)S(1)}, u32[]{:S(2)}, u32[]{:S(2)}) collective-permute-start(f32[224,128]{1,0:T(8,128)S(1)} %get-tuple-element.67), channel_id=1, source_target_pairs={{0,28},{4,0},{8,4},{12,8},{16,12},{20,16},{24,20},{28,24},{1,29},{... | collective-permute-start | bytes 344072 | tf_op jit(solution)/shard_map/ppermute | solution.py:768
  15.5 15.6 %collective-permute-start.2 = (f32[176,128]{1,0:T(8,128)S(1)}, f32[176,128]{1,0:T(8,128)S(1)}, u32[]{:S(2)}, u32[]{:S(2)}) collective-permute-start(f32[176,128]{1,0:T(8,128)S(1)} %get-tuple-element.59), channel_id=1, source_target_pairs={{0,4},{4,8},{8,12},{12,16},{16,20},{20,24},{24,28},{28,0},{1,5},{5... | collective-permute-start | bytes 270344 | tf_op jit(solution)/shard_map/ppermute | solution.py:768
  17.3 13.8 %collective-permute-start.3 = (f32[176,128]{1,0:T(8,128)S(1)}, f32[176,128]{1,0:T(8,128)S(1)}, u32[]{:S(2)}, u32[]{:S(2)}) collective-permute-start(f32[176,128]{1,0:T(8,128)S(1)} %get-tuple-element.60), channel_id=1, source_target_pairs={{0,28},{4,0},{8,4},{12,8},{16,12},{20,16},{24,20},{28,24},{1,29},{... | collective-permute-start | bytes 270344 | tf_op jit(solution)/shard_map/ppermute | solution.py:768
  31.8 11.0 %collective-permute-start.7 = (f32[440,128]{1,0:T(8,128)S(1)}, f32[440,128]{1,0:T(8,128)S(1)}, u32[]{:S(2)}, u32[]{:S(2)}) collective-permute-start(f32[440,128]{1,0:T(8,128)S(1)} %get-tuple-element.71), channel_id=1, source_target_pairs={{0,32},{32,64},{64,96},{96,128},{128,160},{160,192},{192,224},{224... | collective-permute-start | bytes 675848 | tf_op jit(solution)/shard_map/ppermute | solution.py:768
  34.9 7.9 %collective-permute-start.8 = (f32[264,128]{1,0:T(8,128)S(1)}, f32[264,128]{1,0:T(8,128)S(1)}, u32[]{:S(2)}, u32[]{:S(2)}) collective-permute-start(f32[264,128]{1,0:T(8,128)S(1)} %get-tuple-element.72), channel_id=1, source_target_pairs={{0,224},{32,0},{64,32},{96,64},{128,96},{160,128},{192,160},{224,1... | collective-permute-start | bytes 405512 | tf_op jit(solution)/shard_map/ppermute | solution.py:768
  37.5 7.2 %copy-start = (f32[3,8,16,128]{3,2,1,0:T(8,128)S(1)}, f32[3,8,16,128]{3,2,1,0:T(8,128)}, u32[]{:S(2)}) copy-start(f32[3,8,16,128]{3,2,1,0:T(8,128)} %speed.1) | copy-start | bytes 589828
  46.4 2.6 %collective-permute-start.9 = (f32[16,128]{1,0:T(8,128)S(1)}, f32[16,128]{1,0:T(8,128)S(1)}, u32[]{:S(2)}, u32[]{:S(2)}) collective-permute-start(f32[16,128]{1,0:T(8,128)S(1)} %get-tuple-element.81), channel_id=1, source_target_pairs={{0,1},{1,2},{2,3},{3,0},{4,5},{5,6},{6,7},{7,4},{8,9},{9,10},{10,1... | collective-permute-start | bytes 24584 | tf_op jit(solution)/shard_map/ppermute | solution.py:768
  46.5 3.8 %collective-permute-start.10 = (f32[16,128]{1,0:T(8,128)S(1)}, f32[16,128]{1,0:T(8,128)S(1)}, u32[]{:S(2)}, u32[]{:S(2)}) collective-permute-start(f32[16,128]{1,0:T(8,128)S(1)} %get-tuple-element.82), channel_id=1, source_target_pairs={{0,3},{1,0},{2,1},{3,2},{4,7},{5,4},{6,5},{7,6},{8,11},{9,8},{10,9... | collective-permute-start | bytes 24584 | tf_op jit(solution)/shard_map/ppermute | solution.py:768
  50.9 7.6 %collective-permute-start.11 = (f32[80,128]{1,0:T(8,128)S(1)}, f32[80,128]{1,0:T(8,128)S(1)}, u32[]{:S(2)}, u32[]{:S(2)}) collective-permute-start(f32[80,128]{1,0:T(8,128)S(1)} %get-tuple-element.83), channel_id=1, source_target_pairs={{0,4},{4,8},{8,12},{12,16},{16,20},{20,24},{24,28},{28,0},{1,5},{5... | collective-permute-start | bytes 122888 | tf_op jit(solution)/shard_map/ppermute | solution.py:768
  51.0 7.5 %collective-permute-start.12 = (f32[80,128]{1,0:T(8,128)S(1)}, f32[80,128]{1,0:T(8,128)S(1)}, u32[]{:S(2)}, u32[]{:S(2)}) collective-permute-start(f32[80,128]{1,0:T(8,128)S(1)} %get-tuple-element.84), channel_id=1, source_target_pairs={{0,28},{4,0},{8,4},{12,8},{16,12},{20,16},{24,20},{28,24},{1,29},{... | collective-permute-start | bytes 122888 | tf_op jit(solution)/shard_map/ppermute | solution.py:768
  59.1 6.4 %collective-permute-start.13 = (f32[192,128]{1,0:T(8,128)S(1)}, f32[192,128]{1,0:T(8,128)S(1)}, u32[]{:S(2)}, u32[]{:S(2)}) collective-permute-start(f32[192,128]{1,0:T(8,128)S(1)} %get-tuple-element.90), channel_id=1, source_target_pairs={{0,32},{32,64},{64,96},{96,128},{128,160},{160,192},{192,224},{224... | collective-permute-start | bytes 294920 | tf_op jit(solution)/shard_map/ppermute | solution.py:768
  62.6 6.6 %collective-permute-start.14 = (f32[192,128]{1,0:T(8,128)S(1)}, f32[192,128]{1,0:T(8,128)S(1)}, u32[]{:S(2)}, u32[]{:S(2)}) collective-permute-start(f32[192,128]{1,0:T(8,128)S(1)} %get-tuple-element.91), channel_id=1, source_target_pairs={{0,224},{32,0},{64,32},{96,64},{128,96},{160,128},{192,160},{224,1... | collective-permute-start | bytes 294920 | tf_op jit(solution)/shard_map/ppermute | solution.py:768
  70.9 2.6 %collective-permute-start.15 = (f32[16,128]{1,0:T(8,128)S(1)}, f32[16,128]{1,0:T(8,128)S(1)}, u32[]{:S(2)}, u32[]{:S(2)}) collective-permute-start(f32[16,128]{1,0:T(8,128)S(1)} %get-tuple-element.94), channel_id=1, source_target_pairs={{0,1},{1,2},{2,3},{3,0},{4,5},{5,6},{6,7},{7,4},{8,9},{9,10},{10,1... | collective-permute-start | bytes 24584 | tf_op jit(solution)/shard_map/ppermute | solution.py:768
  71.0 3.8 %collective-permute-start.16 = (f32[16,128]{1,0:T(8,128)S(1)}, f32[16,128]{1,0:T(8,128)S(1)}, u32[]{:S(2)}, u32[]{:S(2)}) collective-permute-start(f32[16,128]{1,0:T(8,128)S(1)} %get-tuple-element.95), channel_id=1, source_target_pairs={{0,3},{1,0},{2,1},{3,2},{4,7},{5,4},{6,5},{7,6},{8,11},{9,8},{10,9... | collective-permute-start | bytes 24584 | tf_op jit(solution)/shard_map/ppermute | solution.py:768
  75.3 7.8 %collective-permute-start.17 = (f32[80,128]{1,0:T(8,128)S(1)}, f32[80,128]{1,0:T(8,128)S(1)}, u32[]{:S(2)}, u32[]{:S(2)}) collective-permute-start(f32[80,128]{1,0:T(8,128)S(1)} %get-tuple-element.96), channel_id=1, source_target_pairs={{0,4},{4,8},{8,12},{12,16},{16,20},{20,24},{24,28},{28,0},{1,5},{5... | collective-permute-start | bytes 122888 | tf_op jit(solution)/shard_map/ppermute | solution.py:768
  75.7 7.5 %collective-permute-start.18 = (f32[80,128]{1,0:T(8,128)S(1)}, f32[80,128]{1,0:T(8,128)S(1)}, u32[]{:S(2)}, u32[]{:S(2)}) collective-permute-start(f32[80,128]{1,0:T(8,128)S(1)} %get-tuple-element.97), channel_id=1, source_target_pairs={{0,28},{4,0},{8,4},{12,8},{16,12},{20,16},{24,20},{28,24},{1,29},{... | collective-permute-start | bytes 122888 | tf_op jit(solution)/shard_map/ppermute | solution.py:768
  83.8 5.1 %collective-permute-start.19 = (f32[192,128]{1,0:T(8,128)S(1)}, f32[192,128]{1,0:T(8,128)S(1)}, u32[]{:S(2)}, u32[]{:S(2)}) collective-permute-start(f32[192,128]{1,0:T(8,128)S(1)} %get-tuple-element.103), channel_id=1, source_target_pairs={{0,32},{32,64},{64,96},{96,128},{128,160},{160,192},{192,224},{224... | collective-permute-start | bytes 294920 | tf_op jit(solution)/shard_map/ppermute | solution.py:768
  86.0 6.2 %collective-permute-start.20 = (f32[192,128]{1,0:T(8,128)S(1)}, f32[192,128]{1,0:T(8,128)S(1)}, u32[]{:S(2)}, u32[]{:S(2)}) collective-permute-start(f32[192,128]{1,0:T(8,128)S(1)} %get-tuple-element.104), channel_id=1, source_target_pairs={{0,224},{32,0},{64,32},{96,64},{128,96},{160,128},{192,160},{224,1... | collective-permute-start | bytes 294920 | tf_op jit(solution)/shard_map/ppermute | solution.py:768
where the time goes:
time: 94.6 us; the launch traced here: 94.5 us
  Pallas kernels  46.3 us (49%)
  starting transfers between devices  32.9 us (35%)
  waiting for transfers between devices  14.3 us (15%)
    pallas_call x18, Pallas kernels, call(): pl.pallas_call(kernel, out_shape=[jax.ShapeDtypeStruct(shape, jnp.float32...  42.5 us
    ppermute x21, starting transfers between devices, sent(): lax.ppermute(value, axis, [(i, (i + distance) % count) for i in range(cou...  32.9 us
    ppermute x21, waiting for transfers between devices, sent(): lax.ppermute(value, axis, [(i, (i + distance) % count) for i in range(cou...  14.3 us
    pallas_call x1, Pallas kernels, on_device(): pl.pallas_call(part(start_kernel, extent), out_shape=[pltpu.VMEM(shape, k...  3.86 us
  transfers between devices with their start and end apart: 21, of which 8 were waited for; matrix products, arithmetic and copies ran while one was open for 0% of the time, Pallas kernels for 34%

commit v1 on v0

--- a/solution.py
+++ b/solution.py
@@ -155,6 +155,24 @@
             up = jnp.where(here, rolled(value, lane_of - (LANES - REACH)), up)
             down = jnp.where(here, rolled(value, lane_of), down)
     return up, down
+
+
+class Either:
+    def __init__(self, odd, if_odd, if_even):
+        self.odd, self.if_odd, self.if_even = odd, if_odd, if_even
+
+    def __getitem__(self, rows):
+        return jnp.where(self.odd > 0, self.if_odd[rows], self.if_even[rows])
+
+
+def by_parity(odd, near, far, write):
+    @pl.when(odd > 0)
+    def _():
+        write(far, near)
+
+    @pl.when(odd == 0)
+    def _():
+        write(near, far)
 
 
 def kept(flag, value):
@@ -331,18 +349,22 @@
 
 
 def x_layers_kernel(
-    extent, edges, motion, z_low, z_high, y_low, y_high, x_up, x_down, wide, wide_pack
+    extent, edges, motion, z_low, z_high, y_low, y_high, x_near, x_far, wide, wide_pack
 ):
     widen_fields(
         edges, lambda field, layer: motion[field, layer],
         3, extent, z_low, z_high, y_low, y_high, lambda field: wide.at[field], wide_pack,
     )
-    copy_x_layers(3, extent, lambda field: wide.at[field], wide_pack, x_up, x_down)
+
+    def write(x_up, x_down):
+        copy_x_layers(3, extent, lambda field: wide.at[field], wide_pack, x_up, x_down)
+
+    by_parity(edges[6], x_near, x_far, write)
 
 
 def x_layers_first_kernel(
     extent, edges, motion, stiffness, pore, z_low, z_high, y_low, y_high, rows_low, rows_high,
-    wide_static, wide_pack, wide_broken, x_up, x_down, wide,
+    wide_static, wide_pack, wide_broken, x_near, x_far, wide,
 ):
     size_x, size_y, _ = extent
 
@@ -367,22 +389,26 @@
                 pack[first : first + size_y],
                 y_high[at : at + REACH],
             )
-    at = copy_x_layers(4, extent, target, wide_pack, x_up, x_down)
-    height = wide.shape[2]
-    x_up[at : at + size_y] = pore[size_x - 1]
-    x_down[at : at + size_y] = pore[0]
-    at += size_y
-    for order in range(2):
-        for layer in range(NEAR):
-            x_up[at : at + height] = wide_broken[order, size_x - NEAR + layer]
-            at += height
-    for plane, (a, b, _) in enumerate(OFFSETS):
-        if a * b == 0:
-            continue
-        rows, many = abs(b), a * abs(b)
-        source = rows_low if b > 0 else rows_high
-        first = PAD + (Y_UP if b > 0 else Y_DOWN)[plane] * size_x + (size_x - a) * rows
-        x_up[at + XY_UP[plane] : at + XY_UP[plane] + many] = source[first : first + many]
+
+    def write(x_up, x_down):
+        at = copy_x_layers(4, extent, target, wide_pack, x_up, x_down)
+        height = wide.shape[2]
+        x_up[at : at + size_y] = pore[size_x - 1]
+        x_down[at : at + size_y] = pore[0]
+        at += size_y
+        for order in range(2):
+            for layer in range(NEAR):
+                x_up[at : at + height] = wide_broken[order, size_x - NEAR + layer]
+                at += height
+        for plane, (a, b, _) in enumerate(OFFSETS):
+            if a * b == 0:
+                continue
+            rows, many = abs(b), a * abs(b)
+            source = rows_low if b > 0 else rows_high
+            first = PAD + (Y_UP if b > 0 else Y_DOWN)[plane] * size_x + (size_x - a) * rows
+            x_up[at + XY_UP[plane] : at + XY_UP[plane] + many] = source[first : first + many]
+
+    by_parity(edges[6], x_near, x_far, write)
 
 
 def each_shift(main, beside, add_step, reach=REACH):
@@ -532,7 +558,7 @@
 
 
 def weights_outer_kernel(
-    extent, edges, stiffness, pore, wide, wide_pack, x_up, x_broken, x_low, x_high,
+    extent, edges, stiffness, pore, wide, wide_pack, x_up, x_broken, x_far, x_near,
     weights, pressing, shifts, planes, besides,
 ):
     size_x, size_y, _ = extent
@@ -540,6 +566,8 @@
     pore_at = x_place(4, REACH, size_y) + height
     broken_at = pore_at + size_y
     rows_at = broken_at + 2 * NEAR * height
+    x_low = Either(edges[6], x_near, x_far)
+    x_high = Either(edges[6], x_far, x_near)
     fill_outer(extent, 4, edges, (3,), x_low, x_high, shifts, besides)
     for plane, (a, b, _) in enumerate(OFFSETS):
         for layer in range(a):
@@ -705,7 +733,7 @@
 
 
 def finish_kernel(
-    extent, count, stage, edges, motion, speed, pressing, inner, weights, x_low, x_high, *refs
+    extent, count, stage, edges, motion, speed, pressing, inner, weights, x_far, x_near, *refs
 ):
     size_x, size_y, _ = extent
     if stage == "last":
@@ -713,6 +741,8 @@
     else:
         motion_out, speed_out, z_up, z_down, total, shifts, besides = refs
     total[...] = inner[...] + pressing[...]
+    x_low = Either(edges[6], x_near, x_far)
+    x_high = Either(edges[6], x_far, x_near)
     fill_outer(extent, count, edges, range(3), x_low, x_high, shifts, besides)
     for step, first, last, bonds, base in outer_plan(extent)[0]:
         for layer in range(first, last):
@@ -768,6 +798,13 @@
     return lax.ppermute(value, axis, [(i, (i + distance) % count) for i in range(count)])
 
 
+def swapped(near, far):
+    count = lax.axis_size("gx")
+    side = [1 - 2 * (i % 2) for i in range(count)]
+    far = lax.ppermute(far, "gx", [(i, (i - side[i]) % count) for i in range(count)])
+    return lax.ppermute(near, "gx", [(i, i + side[i]) for i in range(count)]), far
+
+
 def on_device(displacement, velocity, stiffness, broken, borehole_id, flags, pressure):
     extent = stiffness.shape
     size_x, size_y, _ = extent
@@ -782,6 +819,7 @@
                 (lax.axis_index(axis) < lax.axis_size(axis) - 1).astype(jnp.int32),
             )
         ]
+        + [lax.axis_index("gx") % 2]
     )
     field = (size_x, size_y, LANES)
     vector = (3,) + field
@@ -863,19 +901,19 @@
     early, early_shifts = force_early(motion, z_low, z_high)
     y_low, y_high, x_broken, early = lax.optimization_barrier((y_low, y_high, x_broken, early))
     layers = x_place(4, REACH, size_y) + height + size_y
-    wide_static, wide_pack, wide_broken, x_fields_up, x_fields_down = call(
+    layers = round_up(layers + 2 * NEAR * height + XY_UP_COUNT)
+    wide_static, wide_pack, wide_broken, x_near, x_far = call(
         part(x_layers_first_kernel, extent), [edges],
         [motion, stiffness, pore, z_low, z_high, y_low, y_high, rows_low, rows_high],
         [
             (2, size_x, height, LANES),
             (2, height, LANES),
             (2, size_x, height, LANES),
-            (round_up(layers + 2 * NEAR * height + XY_UP_COUNT), LANES),
-            (round_up(layers), LANES),
+            (layers, LANES),
+            (layers, LANES),
         ], [(3, size_x, height, LANES)], name="x_layers_first",
     )
-    x_low = sent(x_fields_up, "gx", 1)
-    x_high = sent(x_fields_down, "gx", -1)
+    x_near, x_far = swapped(x_near, x_far)
     (weights_late,) = call(
         part(weights_late_kernel, extent), [],
         [stiffness, wide_static, wide_pack, wide_broken, rows_low, rows_high, keeps],
@@ -885,7 +923,7 @@
     inner = force_late(5, motion, early, early_shifts, y_low, y_high)
     outer_weights, pressing = call(
         part(weights_outer_kernel, extent), [edges],
-        [stiffness, pore, wide_static, wide_pack, x_up, x_broken, x_low, x_high],
+        [stiffness, pore, wide_static, wide_pack, x_up, x_broken, x_far, x_near],
         [(outer_slots, 8, LANES), vector],
         [
             (moves, 1, 2 * REACH, height, LANES),
@@ -894,12 +932,12 @@
         ], name="weights_outer",
     )
 
-    def finish(stage, count, motion, speed, inner, x_low, x_high):
+    def finish(stage, count, motion, speed, inner, x_near, x_far):
         columns = (size_y, LANES)
         shapes = [vector] * 3 if stage == "last" else [vector, vector, columns, columns]
         return call(
             part(finish_kernel, extent, count, stage), [edges],
-            [motion, speed, pressing, inner, outer_weights, x_low, x_high],
+            [motion, speed, pressing, inner, outer_weights, x_far, x_near],
             shapes,
             [
                 vector,
@@ -910,7 +948,7 @@
         )
 
     motion, speed, z_up, z_down = finish(
-        "first", 4, motion, velocity, inner, x_low, x_high
+        "first", 4, motion, velocity, inner, x_near, x_far
     )
     for step_index in range(STEPS):
         z_low = sent(z_up, "gz", 1)
@@ -925,19 +963,18 @@
         early, early_shifts = force_early(motion, z_low, z_high)
         y_low, y_high, early = lax.optimization_barrier((y_low, y_high, early))
         layers = round_up(x_place(3, REACH, size_y) + height)
-        x_up, x_down = call(
+        x_near, x_far = call(
             part(x_layers_kernel, extent), [edges],
             [motion, z_low, z_high, y_low, y_high],
             [(layers, LANES), (layers, LANES)],
             [(3, size_x, height, LANES), (2, height, LANES)], name="x_layers",
         )
-        x_low = sent(x_up, "gx", 1)
-        x_high = sent(x_down, "gx", -1)
+        x_near, x_far = swapped(x_near, x_far)
         inner = force_late(3, motion, early, early_shifts, y_low, y_high)
         if step_index < STEPS - 1:
-            motion, speed, z_up, z_down = finish("middle", 3, motion, speed, inner, x_low, x_high)
+            motion, speed, z_up, z_down = finish("middle", 3, motion, speed, inner, x_near, x_far)
         else:
-            motion, speed, accel = finish("last", 3, motion, speed, inner, x_low, x_high)
+            motion, speed, accel = finish("last", 3, motion, speed, inner, x_near, x_far)
     return (motion, speed, accel)
 
 

time: 94.6 us -> 91.5 us (0.967)
  waiting for transfers between devices: 14.3 us -> 5.12 us
  starting transfers between devices: 32.9 us -> 38.1 us
    ppermute x0 -> x6, starting transfers between devices: none -> 12.5 us  [the longest x3 12.5 us: swapped(): lax.ppermute(far, 'gx', [(i, (i - side[i]) % count) for i in range(count)])]
    ppermute x21 -> x15, waiting for transfers between devices: 14.3 us -> 5.1 us  [sent(): lax.ppermute(value, axis, [(i, (i + distance) % count) for i in range(cou...]
    ppermute x21 -> x15, starting transfers between devices: 32.9 us -> 25.6 us  [sent(): lax.ppermute(value, axis, [(i, (i + distance) % count) for i in range(cou...]
  transfers between devices with their start and end apart: 21 -> 21, of which waited for: 8 -> 5; matrix products, arithmetic and copies ran while one was open for 0% -> 0% of each run, Pallas kernels for 34% -> 35%
where the time goes in v1:
time: 91.5 us; the launch traced here: 90.6 us
  Pallas kernels  46.4 us (51%)
  starting transfers between devices  38.1 us (42%)
  waiting for transfers between devices  5.12 us (6%)
    pallas_call x18, Pallas kernels, call(): pl.pallas_call(kernel, out_shape=[jax.ShapeDtypeStruct(shape, jnp.float32...  42.6 us
    ppermute x15, starting transfers between devices, sent(): lax.ppermute(value, axis, [(i, (i + distance) % count) for i in range(cou...  25.6 us
    ppermute x3, starting transfers between devices, swapped(): lax.ppermute(far, 'gx', [(i, (i - side[i]) % count) for i in range(count)])  12.5 us
    ppermute x15, waiting for transfers between devices, sent(): lax.ppermute(value, axis, [(i, (i + distance) % count) for i in range(cou...  5.1 us
    pallas_call x1, Pallas kernels, on_device(): pl.pallas_call(part(start_kernel, extent), out_shape=[pltpu.VMEM(shape, k...  3.86 us
  transfers between devices with their start and end apart: 21, of which 5 were waited for; matrix products, arithmetic and copies ran while one was open for 0% of the time, Pallas kernels for 35%

profile of v1, /device:TPU:71, one launch (start us, length us, event | category | flops | bytes accessed | tf_op | source)
XLA Modules:
  0.0 90.6 jit_solution(11620096372811574509)
XLA Ops:
  0.6 3.9 %start.1 = (f32[3,8,16,128]{3,2,1,0:T(8,128)S(1)}, f32[8,16,128]{2,1,0:T(8,128)S(1)}, f32[8,16,128]{2,1,0:T(8,128)S(1)}, f32[152,128]{1,0:T(8,128)S(1)}, f32[152...) custom-call(f32[8]{0:T(128)} %pressure_in.1, ...), custom_call_target="tpu_custom_call" | custom-call | tf_op jit(solution)/shard_map/start/pallas_call | solution.py:831
  4.5 4.8 %collective-permute-start.4 = (f32[1120,128]{1,0:T(8,128)S(1)}, f32[1120,128]{1,0:T(8,128)S(1)}, u32[]{:S(2)}, u32[]{:S(2)}) collective-permute-start(f32[1120,128]{1,0:T(8,128)S(1)} %get-tuple-element.61.x_up), channel_id=1, source_target_pairs={{0,32},{32,64},{64,96},{96,128},{128,160},{160,192},{192,224},{224... | collective-permute-start | bytes 1720328 | tf_op jit(solution)/shard_map/ppermute | solution.py:798
  9.3 0.7 collective-permute-start.5
  10.3 1.3 %collective-permute-start.1 = (f32[152,128]{1,0:T(8,128)S(1)}, f32[152,128]{1,0:T(8,128)S(1)}, u32[]{:S(2)}, u32[]{:S(2)}) collective-permute-start(f32[152,128]{1,0:T(8,128)S(1)} %get-tuple-element.58), channel_id=1, source_target_pairs={{0,3},{1,0},{2,1},{3,2},{4,7},{5,4},{6,5},{7,6},{8,11},{9,8},{10,9... | collective-permute-start | bytes 233480 | tf_op jit(solution)/shard_map/ppermute | solution.py:798
  11.5 2.8 %collective-permute-start.6 = (f32[224,128]{1,0:T(8,128)S(1)}, f32[224,128]{1,0:T(8,128)S(1)}, u32[]{:S(2)}, u32[]{:S(2)}) collective-permute-start(f32[224,128]{1,0:T(8,128)S(1)} %get-tuple-element.67), channel_id=1, source_target_pairs={{0,28},{4,0},{8,4},{12,8},{16,12},{20,16},{24,20},{28,24},{1,29},{... | collective-permute-start | bytes 344072 | tf_op jit(solution)/shard_map/ppermute | solution.py:798
  15.5 1.8 %collective-permute-start.2 = (f32[176,128]{1,0:T(8,128)S(1)}, f32[176,128]{1,0:T(8,128)S(1)}, u32[]{:S(2)}, u32[]{:S(2)}) collective-permute-start(f32[176,128]{1,0:T(8,128)S(1)} %get-tuple-element.59), channel_id=1, source_target_pairs={{0,4},{4,8},{8,12},{12,16},{16,20},{20,24},{24,28},{28,0},{1,5},{5... | collective-permute-start | bytes 270344 | tf_op jit(solution)/shard_map/ppermute | solution.py:798
  17.3 1.8 %collective-permute-start.3 = (f32[176,128]{1,0:T(8,128)S(1)}, f32[176,128]{1,0:T(8,128)S(1)}, u32[]{:S(2)}, u32[]{:S(2)}) collective-permute-start(f32[176,128]{1,0:T(8,128)S(1)} %get-tuple-element.60), channel_id=1, source_target_pairs={{0,28},{4,0},{8,4},{12,8},{16,12},{20,16},{24,20},{28,24},{1,29},{... | collective-permute-start | bytes 270344 | tf_op jit(solution)/shard_map/ppermute | solution.py:798
  19.1 7.9 %weights_early.1 = (f32[1024,8,128]{2,1,0:T(8,128)S(1)}, f32[648,8,128]{2,1,0:T(8,128)S(1)}) custom-call(s32[7]{0:T(128)S(1)} %stack.55.edges, s32[61,8,16,128]{3,2,1,0:T(8,128)} %broken_in.3, f32[8,16,128]{2,1,0:T(8,128)S(1)} %get-tuple-element.55.stiffness, f32[152,128]{1,0:T(8,128)S(1)} %collective-permute-done.z_low, ...), custom_call_target="tpu_custom_call" | custom-call | tf_op jit(solution)/shard_map/weights_early/pallas_call | solution.py:776
  27.0 4.0 %force_early.3 = (f32[3,8,16,128]{3,2,1,0:T(8,128)S(1)}, f32[7,3,8,32,128]{4,3,2,1,0:T(8,128)S(1)}) custom-call(s32[7]{0:T(128)S(1)} %stack.55.edges, f32[3,8,16,128]{3,2,1,0:T(8,128)S(1)} %get-tuple-element.54.motion, f32[152,128]{1,0:T(8,128)S(1)} %collective-permute-done.z_low, f32[152,128]{1,0:T(8,128)S(1)} %collective-permute-done.1.z_high, ...), custom_call_target="tpu_custom_call" | custom-call | tf_op jit(solution)/shard_map/force_early/pallas_call | solution.py:776
  31.1 0.7 x_layers_first.1
  31.8 3.1 %collective-permute-start.7 = (f32[440,128]{1,0:T(8,128)S(1)}, f32[440,128]{1,0:T(8,128)S(1)}, u32[]{:S(2)}, u32[]{:S(2)}) collective-permute-start(f32[440,128]{1,0:T(8,128)S(1)} %get-tuple-element.71), channel_id=1, source_target_pairs={{0,224},{32,64},{64,32},{96,128},{128,96},{160,192},{192,160},{224... | collective-permute-start | bytes 675848 | tf_op jit(solution)/shard_map/ppermute | solution.py:804
  34.8 2.6 %weights_late.1.weights = f32[648,8,128]{2,1,0:T(8,128)S(1)} custom-call(f32[8,16,128]{2,1,0:T(8,128)S(1)} %get-tuple-element.55.stiffness, f32[2,8,24,128]{3,2,1,0:T(8,128)S(1)} %get-tuple-element.68.wide, f32[2,24,128]{2,1,0:T(8,128)S(1)} %get-tuple-element.69.wide_pack, f32[2,8,24,128]{3,2,1,0:T(8,128)S(1)} %get-tuple-element.76.wide_broken, ...), custom_call_target="tpu_custom_call" | custom-call | tf_op jit(solution)/shard_map/weights_late/pallas_call | solution.py:776
  37.5 2.9 %force_late.3.inner = f32[3,8,16,128]{3,2,1,0:T(8,128)S(1)} custom-call(s32[7]{0:T(128)S(1)} %stack.55.edges, f32[3,8,16,128]{3,2,1,0:T(8,128)S(1)} %get-tuple-element.54.motion, f32[3,8,16,128]{3,2,1,0:T(8,128)S(1)} %get-tuple-element.74.early, f32[7,3,8,32,128]{4,3,2,1,0:T(8,128)S(1)} %get-tuple-element.75.early_shifts, ...), custom_call_target="tpu_custom_call" | custom-call | tf_op jit(solution)/shard_map/force_late/pallas_call | solution.py:776
  40.4 1.9 %weights_outer.1 = (f32[280,8,128]{2,1,0:T(8,128)S(1)}, f32[3,8,16,128]{3,2,1,0:T(8,128)S(1)}) custom-call(s32[7]{0:T(128)S(1)} %stack.55.edges, f32[8,16,128]{2,1,0:T(8,128)S(1)} %get-tuple-element.55.stiffness, f32[8,16,128]{2,1,0:T(8,128)S(1)} %get-tuple-element.56.pore, f32[2,8,24,128]{3,2,1,0:T(8,128)S(1)} %get-tuple-element.68.wide, ...), custom_call_target="tpu_custom_call" | custom-call | tf_op jit(solution)/shard_map/weights_outer/pallas_call | solution.py:776
  42.4 1.7 %finish_first.1 = (f32[3,8,16,128]{3,2,1,0:T(8,128)S(1)}, f32[3,8,16,128]{3,2,1,0:T(8,128)S(1)}, f32[16,128]{1,0:T(8,128)S(1)}, f32[16,128]{1,0:T(8,128)S(1)}) custom-call(s32[7]{0:T(128)S(1)} %stack.55.edges, f32[3,8,16,128]{3,2,1,0:T(8,128)S(1)} %get-tuple-element.54.motion, f32[3,8,16,128]{3,2,1,0:T(8,128)S(1)} %copy-done, ...), custom_call_target="tpu_custom_call" | custom-call | tf_op jit(solution)/shard_map/finish_first/pallas_call | solution.py:776
  44.2 1.5 %collective-permute-start.10 = (f32[16,128]{1,0:T(8,128)S(1)}, f32[16,128]{1,0:T(8,128)S(1)}, u32[]{:S(2)}, u32[]{:S(2)}) collective-permute-start(f32[16,128]{1,0:T(8,128)S(1)} %get-tuple-element.82), channel_id=1, source_target_pairs={{0,3},{1,0},{2,1},{3,2},{4,7},{5,4},{6,5},{7,6},{8,11},{9,8},{10,9... | collective-permute-start | bytes 24584 | tf_op jit(solution)/shard_map/ppermute | solution.py:798
  45.6 1.0 %collective-permute-done.9.z_low = f32[16,128]{1,0:T(8,128)S(1)} collective-permute-done((f32[16,128]{1,0:T(8,128)S(1)}, f32[16,128]{1,0:T(8,128)S(1)}, u32[]{:S(2)}, u32[]{:S(2)}) %collective-permute-start.9) | collective-permute-done | bytes 8224 | tf_op jit(solution)/shard_map/ppermute | solution.py:798
  46.7 1.3 %collective-permute-done.10.z_high = f32[16,128]{1,0:T(8,128)S(1)} collective-permute-done((f32[16,128]{1,0:T(8,128)S(1)}, f32[16,128]{1,0:T(8,128)S(1)}, u32[]{:S(2)}, u32[]{:S(2)}) %collective-permute-start.10) | collective-permute-done | bytes 8224 | tf_op jit(solution)/shard_map/ppermute | solution.py:798
  48.5 2.9 %collective-permute-start.11 = (f32[80,128]{1,0:T(8,128)S(1)}, f32[80,128]{1,0:T(8,128)S(1)}, u32[]{:S(2)}, u32[]{:S(2)}) collective-permute-start(f32[80,128]{1,0:T(8,128)S(1)} %get-tuple-element.83), channel_id=1, source_target_pairs={{0,4},{4,8},{8,12},{12,16},{16,20},{20,24},{24,28},{28,0},{1,5},{5... | collective-permute-start | bytes 122888 | tf_op jit(solution)/shard_map/ppermute | solution.py:798
  51.5 2.2 %collective-permute-start.12 = (f32[80,128]{1,0:T(8,128)S(1)}, f32[80,128]{1,0:T(8,128)S(1)}, u32[]{:S(2)}, u32[]{:S(2)}) collective-permute-start(f32[80,128]{1,0:T(8,128)S(1)} %get-tuple-element.84), channel_id=1, source_target_pairs={{0,28},{4,0},{8,4},{12,8},{16,12},{20,16},{24,20},{28,24},{1,29},{... | collective-permute-start | bytes 122888 | tf_op jit(solution)/shard_map/ppermute | solution.py:798
  53.7 4.0 %force_early.4 = (f32[3,8,16,128]{3,2,1,0:T(8,128)S(1)}, f32[7,3,8,32,128]{4,3,2,1,0:T(8,128)S(1)}) custom-call(s32[7]{0:T(128)S(1)} %stack.55.edges, f32[3,8,16,128]{3,2,1,0:T(8,128)S(1)} %get-tuple-element.79.motion, f32[16,128]{1,0:T(8,128)S(1)} %collective-permute-done.9.z_low, f32[16,128]{1,0:T(8,128)S(1)} %collective-permute-done.10.z_high, ...), custom_call_target="tpu_custom_call" | custom-call | tf_op jit(solution)/shard_map/force_early/pallas_call | solution.py:776
  58.3 4.3 %collective-permute-start.13 = (f32[192,128]{1,0:T(8,128)S(1)}, f32[192,128]{1,0:T(8,128)S(1)}, u32[]{:S(2)}, u32[]{:S(2)}) collective-permute-start(f32[192,128]{1,0:T(8,128)S(1)} %get-tuple-element.90), channel_id=1, source_target_pairs={{0,224},{32,64},{64,32},{96,128},{128,96},{160,192},{192,160},{224... | collective-permute-start | bytes 294920 | tf_op jit(solution)/shard_map/ppermute | solution.py:804
  62.6 2.9 %force_late.4.inner = f32[3,8,16,128]{3,2,1,0:T(8,128)S(1)} custom-call(s32[7]{0:T(128)S(1)} %stack.55.edges, f32[3,8,16,128]{3,2,1,0:T(8,128)S(1)} %get-tuple-element.79.motion, f32[3,8,16,128]{3,2,1,0:T(8,128)S(1)} %get-tuple-element.86.early, f32[7,3,8,32,128]{4,3,2,1,0:T(8,128)S(1)} %get-tuple-element.87.early_shifts, ...), custom_call_target="tpu_custom_call" | custom-call | tf_op jit(solution)/shard_map/force_late/pallas_call | solution.py:776
  65.5 1.7 %finish_middle.1 = (f32[3,8,16,128]{3,2,1,0:T(8,128)S(1)}, f32[3,8,16,128]{3,2,1,0:T(8,128)S(1)}, f32[16,128]{1,0:T(8,128)S(1)}, f32[16,128]{1,0:T(8,128)S(1)}) custom-call(s32[7]{0:T(128)S(1)} %stack.55.edges, f32[3,8,16,128]{3,2,1,0:T(8,128)S(1)} %get-tuple-element.79.motion, f32[3,8,16,128]{3,2,1,0:T(8,128)S(1)} %get-tuple-element.80.speed, ...), custom_call_target="tpu_custom_call" | custom-call | tf_op jit(solution)/shard_map/finish_middle/pallas_call | solution.py:776
  67.3 1.5 %collective-permute-start.16 = (f32[16,128]{1,0:T(8,128)S(1)}, f32[16,128]{1,0:T(8,128)S(1)}, u32[]{:S(2)}, u32[]{:S(2)}) collective-permute-start(f32[16,128]{1,0:T(8,128)S(1)} %get-tuple-element.95), channel_id=1, source_target_pairs={{0,3},{1,0},{2,1},{3,2},{4,7},{5,4},{6,5},{7,6},{8,11},{9,8},{10,9... | collective-permute-start | bytes 24584 | tf_op jit(solution)/shard_map/ppermute | solution.py:798
  68.8 1.0 %collective-permute-done.15.z_low = f32[16,128]{1,0:T(8,128)S(1)} collective-permute-done((f32[16,128]{1,0:T(8,128)S(1)}, f32[16,128]{1,0:T(8,128)S(1)}, u32[]{:S(2)}, u32[]{:S(2)}) %collective-permute-start.15) | collective-permute-done | bytes 8224 | tf_op jit(solution)/shard_map/ppermute | solution.py:798
  69.8 1.3 %collective-permute-done.16.z_high = f32[16,128]{1,0:T(8,128)S(1)} collective-permute-done((f32[16,128]{1,0:T(8,128)S(1)}, f32[16,128]{1,0:T(8,128)S(1)}, u32[]{:S(2)}, u32[]{:S(2)}) %collective-permute-start.16) | collective-permute-done | bytes 8224 | tf_op jit(solution)/shard_map/ppermute | solution.py:798
  72.0 3.6 %collective-permute-start.18 = (f32[80,128]{1,0:T(8,128)S(1)}, f32[80,128]{1,0:T(8,128)S(1)}, u32[]{:S(2)}, u32[]{:S(2)}) collective-permute-start(f32[80,128]{1,0:T(8,128)S(1)} %get-tuple-element.97), channel_id=1, source_target_pairs={{0,28},{4,0},{8,4},{12,8},{16,12},{20,16},{24,20},{28,24},{1,29},{... | collective-permute-start | bytes 122888 | tf_op jit(solution)/shard_map/ppermute | solution.py:798
  75.6 4.0 %force_early.5 = (f32[3,8,16,128]{3,2,1,0:T(8,128)S(1)}, f32[7,3,8,32,128]{4,3,2,1,0:T(8,128)S(1)}) custom-call(s32[7]{0:T(128)S(1)} %stack.55.edges, f32[3,8,16,128]{3,2,1,0:T(8,128)S(1)} %get-tuple-element.92.motion, f32[16,128]{1,0:T(8,128)S(1)} %collective-permute-done.15.z_low, f32[16,128]{1,0:T(8,128)S(1)} %collective-permute-done.16.z_high, ...), custom_call_target="tpu_custom_call" | custom-call | tf_op jit(solution)/shard_map/force_early/pallas_call | solution.py:776
  80.2 5.1 %collective-permute-start.19 = (f32[192,128]{1,0:T(8,128)S(1)}, f32[192,128]{1,0:T(8,128)S(1)}, u32[]{:S(2)}, u32[]{:S(2)}) collective-permute-start(f32[192,128]{1,0:T(8,128)S(1)} %get-tuple-element.103), channel_id=1, source_target_pairs={{0,224},{32,64},{64,32},{96,128},{128,96},{160,192},{192,160},{224... | collective-permute-start | bytes 294920 | tf_op jit(solution)/shard_map/ppermute | solution.py:804
  85.3 2.9 %force_late.5.inner = f32[3,8,16,128]{3,2,1,0:T(8,128)S(1)} custom-call(s32[7]{0:T(128)S(1)} %stack.55.edges, f32[3,8,16,128]{3,2,1,0:T(8,128)S(1)} %get-tuple-element.92.motion, f32[3,8,16,128]{3,2,1,0:T(8,128)S(1)} %get-tuple-element.99.early, f32[7,3,8,32,128]{4,3,2,1,0:T(8,128)S(1)} %get-tuple-element.100.early_shifts, ...), custom_call_target="tpu_custom_call" | custom-call | tf_op jit(solution)/shard_map/force_late/pallas_call | solution.py:776
  88.3 2.3 %finish_last.1 = (f32[3,8,16,128]{3,2,1,0:T(8,128)}, f32[3,8,16,128]{3,2,1,0:T(8,128)}, f32[3,8,16,128]{3,2,1,0:T(8,128)}) custom-call(s32[7]{0:T(128)S(1)} %stack.55.edges, f32[3,8,16,128]{3,2,1,0:T(8,128)S(1)} %get-tuple-element.92.motion, f32[3,8,16,128]{3,2,1,0:T(8,128)S(1)} %get-tuple-element.93.speed, ...), custom_call_target="tpu_custom_call" | custom-call | tf_op jit(solution)/shard_map/finish_last/pallas_call | solution.py:776
  (32 shorter events, 4.2 us)
Async XLA Ops:
  4.5 26.5 %collective-permute-start.4 = (f32[1120,128]{1,0:T(8,128)S(1)}, f32[1120,128]{1,0:T(8,128)S(1)}, u32[]{:S(2)}, u32[]{:S(2)}) collective-permute-start(f32[1120,128]{1,0:T(8,128)S(1)} %get-tuple-element.61.x_up), channel_id=1, source_target_pairs={{0,32},{32,64},{64,96},{96,128},{128,160},{160,192},{192,224},{224... | collective-permute-start | bytes 1720328 | tf_op jit(solution)/shard_map/ppermute | solution.py:798
  9.3 21.7 %collective-permute-start.5 = (f32[368,128]{1,0:T(8,128)S(1)}, f32[368,128]{1,0:T(8,128)S(1)}, u32[]{:S(2)}, u32[]{:S(2)}) collective-permute-start(f32[368,128]{1,0:T(8,128)S(1)} %get-tuple-element.66), channel_id=1, source_target_pairs={{0,4},{4,8},{8,12},{12,16},{16,20},{20,24},{24,28},{28,0},{1,5},{5... | collective-permute-start | bytes 565256 | tf_op jit(solution)/shard_map/ppermute | solution.py:798
  10.1 4.4 %collective-permute-start = (f32[152,128]{1,0:T(8,128)S(1)}, f32[152,128]{1,0:T(8,128)S(1)}, u32[]{:S(2)}, u32[]{:S(2)}) collective-permute-start(f32[152,128]{1,0:T(8,128)S(1)} %get-tuple-element.57), channel_id=1, source_target_pairs={{0,1},{1,2},{2,3},{3,0},{4,5},{5,6},{6,7},{7,4},{8,9},{9,10},{10,1... | collective-permute-start | bytes 233480 | tf_op jit(solution)/shard_map/ppermute | solution.py:798
  10.3 4.6 %collective-permute-start.1 = (f32[152,128]{1,0:T(8,128)S(1)}, f32[152,128]{1,0:T(8,128)S(1)}, u32[]{:S(2)}, u32[]{:S(2)}) collective-permute-start(f32[152,128]{1,0:T(8,128)S(1)} %get-tuple-element.58), channel_id=1, source_target_pairs={{0,3},{1,0},{2,1},{3,2},{4,7},{5,4},{6,5},{7,6},{8,11},{9,8},{10,9... | collective-permute-start | bytes 233480 | tf_op jit(solution)/shard_map/ppermute | solution.py:798
  11.5 19.5 %collective-permute-start.6 = (f32[224,128]{1,0:T(8,128)S(1)}, f32[224,128]{1,0:T(8,128)S(1)}, u32[]{:S(2)}, u32[]{:S(2)}) collective-permute-start(f32[224,128]{1,0:T(8,128)S(1)} %get-tuple-element.67), channel_id=1, source_target_pairs={{0,28},{4,0},{8,4},{12,8},{16,12},{20,16},{24,20},{28,24},{1,29},{... | collective-permute-start | bytes 344072 | tf_op jit(solution)/shard_map/ppermute | solution.py:798
  15.5 15.5 %collective-permute-start.2 = (f32[176,128]{1,0:T(8,128)S(1)}, f32[176,128]{1,0:T(8,128)S(1)}, u32[]{:S(2)}, u32[]{:S(2)}) collective-permute-start(f32[176,128]{1,0:T(8,128)S(1)} %get-tuple-element.59), channel_id=1, source_target_pairs={{0,4},{4,8},{8,12},{12,16},{16,20},{20,24},{24,28},{28,0},{1,5},{5... | collective-permute-start | bytes 270344 | tf_op jit(solution)/shard_map/ppermute | solution.py:798
  17.3 13.7 %collective-permute-start.3 = (f32[176,128]{1,0:T(8,128)S(1)}, f32[176,128]{1,0:T(8,128)S(1)}, u32[]{:S(2)}, u32[]{:S(2)}) collective-permute-start(f32[176,128]{1,0:T(8,128)S(1)} %get-tuple-element.60), channel_id=1, source_target_pairs={{0,28},{4,0},{8,4},{12,8},{16,12},{20,16},{24,20},{28,24},{1,29},{... | collective-permute-start | bytes 270344 | tf_op jit(solution)/shard_map/ppermute | solution.py:798
  31.8 8.7 %collective-permute-start.7 = (f32[440,128]{1,0:T(8,128)S(1)}, f32[440,128]{1,0:T(8,128)S(1)}, u32[]{:S(2)}, u32[]{:S(2)}) collective-permute-start(f32[440,128]{1,0:T(8,128)S(1)} %get-tuple-element.71), channel_id=1, source_target_pairs={{0,224},{32,64},{64,32},{96,128},{128,96},{160,192},{192,160},{224... | collective-permute-start | bytes 675848 | tf_op jit(solution)/shard_map/ppermute | solution.py:804
  34.8 5.6 %collective-permute-start.8 = (f32[440,128]{1,0:T(8,128)S(1)}, f32[440,128]{1,0:T(8,128)S(1)}, u32[]{:S(2)}, u32[]{:S(2)}) collective-permute-start(f32[440,128]{1,0:T(8,128)S(1)} %get-tuple-element.72), channel_id=1, source_target_pairs={{0,32},{32,0},{64,96},{96,64},{128,160},{160,128},{192,224},{224,1... | collective-permute-start | bytes 675848 | tf_op jit(solution)/shard_map/ppermute | solution.py:805
  37.5 4.9 %copy-start = (f32[3,8,16,128]{3,2,1,0:T(8,128)S(1)}, f32[3,8,16,128]{3,2,1,0:T(8,128)}, u32[]{:S(2)}) copy-start(f32[3,8,16,128]{3,2,1,0:T(8,128)} %speed.1) | copy-start | bytes 589828
  44.1 2.6 %collective-permute-start.9 = (f32[16,128]{1,0:T(8,128)S(1)}, f32[16,128]{1,0:T(8,128)S(1)}, u32[]{:S(2)}, u32[]{:S(2)}) collective-permute-start(f32[16,128]{1,0:T(8,128)S(1)} %get-tuple-element.81), channel_id=1, source_target_pairs={{0,1},{1,2},{2,3},{3,0},{4,5},{5,6},{6,7},{7,4},{8,9},{9,10},{10,1... | collective-permute-start | bytes 24584 | tf_op jit(solution)/shard_map/ppermute | solution.py:798
  44.2 3.8 %collective-permute-start.10 = (f32[16,128]{1,0:T(8,128)S(1)}, f32[16,128]{1,0:T(8,128)S(1)}, u32[]{:S(2)}, u32[]{:S(2)}) collective-permute-start(f32[16,128]{1,0:T(8,128)S(1)} %get-tuple-element.82), channel_id=1, source_target_pairs={{0,3},{1,0},{2,1},{3,2},{4,7},{5,4},{6,5},{7,6},{8,11},{9,8},{10,9... | collective-permute-start | bytes 24584 | tf_op jit(solution)/shard_map/ppermute | solution.py:798
  48.5 9.1 %collective-permute-start.11 = (f32[80,128]{1,0:T(8,128)S(1)}, f32[80,128]{1,0:T(8,128)S(1)}, u32[]{:S(2)}, u32[]{:S(2)}) collective-permute-start(f32[80,128]{1,0:T(8,128)S(1)} %get-tuple-element.83), channel_id=1, source_target_pairs={{0,4},{4,8},{8,12},{12,16},{16,20},{20,24},{24,28},{28,0},{1,5},{5... | collective-permute-start | bytes 122888 | tf_op jit(solution)/shard_map/ppermute | solution.py:798
  51.5 6.2 %collective-permute-start.12 = (f32[80,128]{1,0:T(8,128)S(1)}, f32[80,128]{1,0:T(8,128)S(1)}, u32[]{:S(2)}, u32[]{:S(2)}) collective-permute-start(f32[80,128]{1,0:T(8,128)S(1)} %get-tuple-element.84), channel_id=1, source_target_pairs={{0,28},{4,0},{8,4},{12,8},{16,12},{20,16},{24,20},{28,24},{1,29},{... | collective-permute-start | bytes 122888 | tf_op jit(solution)/shard_map/ppermute | solution.py:798
  58.3 7.2 %collective-permute-start.13 = (f32[192,128]{1,0:T(8,128)S(1)}, f32[192,128]{1,0:T(8,128)S(1)}, u32[]{:S(2)}, u32[]{:S(2)}) collective-permute-start(f32[192,128]{1,0:T(8,128)S(1)} %get-tuple-element.90), channel_id=1, source_target_pairs={{0,224},{32,64},{64,32},{96,128},{128,96},{160,192},{192,160},{224... | collective-permute-start | bytes 294920 | tf_op jit(solution)/shard_map/ppermute | solution.py:804
  62.6 3.0 %collective-permute-start.14 = (f32[192,128]{1,0:T(8,128)S(1)}, f32[192,128]{1,0:T(8,128)S(1)}, u32[]{:S(2)}, u32[]{:S(2)}) collective-permute-start(f32[192,128]{1,0:T(8,128)S(1)} %get-tuple-element.91), channel_id=1, source_target_pairs={{0,32},{32,0},{64,96},{96,64},{128,160},{160,128},{192,224},{224,1... | collective-permute-start | bytes 294920 | tf_op jit(solution)/shard_map/ppermute | solution.py:805
  67.3 2.6 %collective-permute-start.15 = (f32[16,128]{1,0:T(8,128)S(1)}, f32[16,128]{1,0:T(8,128)S(1)}, u32[]{:S(2)}, u32[]{:S(2)}) collective-permute-start(f32[16,128]{1,0:T(8,128)S(1)} %get-tuple-element.94), channel_id=1, source_target_pairs={{0,1},{1,2},{2,3},{3,0},{4,5},{5,6},{6,7},{7,4},{8,9},{9,10},{10,1... | collective-permute-start | bytes 24584 | tf_op jit(solution)/shard_map/ppermute | solution.py:798
  67.3 3.8 %collective-permute-start.16 = (f32[16,128]{1,0:T(8,128)S(1)}, f32[16,128]{1,0:T(8,128)S(1)}, u32[]{:S(2)}, u32[]{:S(2)}) collective-permute-start(f32[16,128]{1,0:T(8,128)S(1)} %get-tuple-element.95), channel_id=1, source_target_pairs={{0,3},{1,0},{2,1},{3,2},{4,7},{5,4},{6,5},{7,6},{8,11},{9,8},{10,9... | collective-permute-start | bytes 24584 | tf_op jit(solution)/shard_map/ppermute | solution.py:798
  71.7 7.8 %collective-permute-start.17 = (f32[80,128]{1,0:T(8,128)S(1)}, f32[80,128]{1,0:T(8,128)S(1)}, u32[]{:S(2)}, u32[]{:S(2)}) collective-permute-start(f32[80,128]{1,0:T(8,128)S(1)} %get-tuple-element.96), channel_id=1, source_target_pairs={{0,4},{4,8},{8,12},{12,16},{16,20},{20,24},{24,28},{28,0},{1,5},{5... | collective-permute-start | bytes 122888 | tf_op jit(solution)/shard_map/ppermute | solution.py:798
  72.0 7.5 %collective-permute-start.18 = (f32[80,128]{1,0:T(8,128)S(1)}, f32[80,128]{1,0:T(8,128)S(1)}, u32[]{:S(2)}, u32[]{:S(2)}) collective-permute-start(f32[80,128]{1,0:T(8,128)S(1)} %get-tuple-element.97), channel_id=1, source_target_pairs={{0,28},{4,0},{8,4},{12,8},{16,12},{20,16},{24,20},{28,24},{1,29},{... | collective-permute-start | bytes 122888 | tf_op jit(solution)/shard_map/ppermute | solution.py:798
  80.2 8.1 %collective-permute-start.19 = (f32[192,128]{1,0:T(8,128)S(1)}, f32[192,128]{1,0:T(8,128)S(1)}, u32[]{:S(2)}, u32[]{:S(2)}) collective-permute-start(f32[192,128]{1,0:T(8,128)S(1)} %get-tuple-element.103), channel_id=1, source_target_pairs={{0,224},{32,64},{64,32},{96,128},{128,96},{160,192},{192,160},{224... | collective-permute-start | bytes 294920 | tf_op jit(solution)/shard_map/ppermute | solution.py:804
  85.3 2.9 %collective-permute-start.20 = (f32[192,128]{1,0:T(8,128)S(1)}, f32[192,128]{1,0:T(8,128)S(1)}, u32[]{:S(2)}, u32[]{:S(2)}) collective-permute-start(f32[192,128]{1,0:T(8,128)S(1)} %get-tuple-element.104), channel_id=1, source_target_pairs={{0,32},{32,0},{64,96},{96,64},{128,160},{160,128},{192,224},{224,1... | collective-permute-start | bytes 294920 | tf_op jit(solution)/shard_map/ppermute | solution.py:805

commit v2 on v1

--- a/solution.py
+++ b/solution.py
@@ -512,11 +512,33 @@
             lax.fori_loop(first, last, one_layer, 0)
 
 
+def pressed(inside, level, own, sign):
+    return jnp.where(inside > 0.0, (-0.5 * sign) * (level - own), 0.0)
+
+
 def weights_late_kernel(
-    extent, stiffness, wide, wide_pack, wide_broken, rows_low, rows_high, keeps, weights,
-    shifts, besides,
+    extent, stiffness, pore, wide, wide_pack, wide_broken, rows_low, rows_high, keeps,
+    weights, pressing, shifts, besides,
 ):
     size_x, size_y, _ = extent
+    middle = slice(REACH, REACH + size_y)
+    for layer in range(size_x):
+        own = pore[layer]
+        besides_z = [
+            beside_columns(wide_pack[0, middle], wide_pack[1, middle], layer * SLOT + field * REACH)
+            for field in (3, 4)
+        ]
+        total = [jnp.zeros((size_y, LANES), jnp.float32) for axis in range(3)]
+        for sign in (1, -1):
+            if 0 <= layer + sign < size_x:
+                pair = wide[0, layer + sign, middle], wide[1, layer + sign, middle]
+                total[0] = total[0] + pressed(*pair, own, sign)
+            rows = slice(REACH + sign, REACH + sign + size_y)
+            total[1] = total[1] + pressed(wide[0, layer, rows], wide[1, layer, rows], own, sign)
+            pair = [moved(wide[order, layer, middle], besides_z[order], sign) for order in range(2)]
+            total[2] = total[2] + pressed(*pair, own, sign)
+        for axis in range(3):
+            pressing[axis, layer] = total[axis]
     for layer in range(size_x):
         besides[layer] = beside_columns(wide_pack[0], wide_pack[1], layer * SLOT + 3 * REACH)
     for layer in range(size_x):
@@ -559,7 +581,7 @@
 
 def weights_outer_kernel(
     extent, edges, stiffness, pore, wide, wide_pack, x_up, x_broken, x_far, x_near,
-    weights, pressing, shifts, planes, besides,
+    pressing_inner, weights, pressing, shifts, planes, besides,
 ):
     size_x, size_y, _ = extent
     height = wide.shape[2]
@@ -603,43 +625,18 @@
                 value = keep * (0.5 * C_BOND) * (stiffness[layer, rows] + far)
                 weights[slot + order] = jnp.where(far > 0.0, value, 0.0)
 
-    middle = slice(REACH, REACH + size_y)
-
-    def wide_field(field, layer):
-        if layer < 0 or layer >= size_x:
-            source = x_low if layer < 0 else x_high
-            at = x_place(field, 1, size_y) + reach_beside(1) if field == 3 else pore_at
-            return kept(edges[4 if layer < 0 else 5], source[at : at + size_y])
-        return wide[field - 3, layer, middle]
-
-    for layer in range(size_x):
-        own = pore[layer]
-        for axis in range(3):
-            total = jnp.zeros((size_y, LANES), jnp.float32)
-            for sign in (1, -1):
-                if axis == 0:
-                    inside = wide_field(3, layer + sign)
-                    level = wide_field(4, layer + sign)
-                elif axis == 1:
-                    rows = slice(REACH + sign, REACH + sign + size_y)
-                    inside = wide[0, layer, rows]
-                    level = wide[1, layer, rows]
-                else:
-                    inside, level = (
-                        moved(
-                            wide[field - 3, layer],
-                            beside_columns(
-                                wide_pack[0], wide_pack[1], layer * SLOT + field * REACH
-                            ),
-                            sign,
-                        )[middle]
-                        for field in (3, 4)
-                    )
-                total = total + jnp.where(inside > 0.0, (-0.5 * sign) * (level - own), 0.0)
-            pressing[axis, layer] = total
-
-
-def add_bonds(bonds, step, layer, far_layer, first_row, motion, shifts, weights, slot, total):
+    at = x_place(3, 1, size_y) + reach_beside(1)
+    pressing[...] = pressing_inner[...]
+    for source, flag, layer, sign in ((x_low, 4, 0, -1), (x_high, 5, size_x - 1, 1)):
+        pressing[0, layer] += pressed(
+            kept(edges[flag], source[at : at + size_y]),
+            source[pore_at : pore_at + size_y], pore[layer], sign,
+        )
+
+
+def add_bonds(
+    bonds, step, layer, far_layer, first_row, motion, shifts, weights, slot, total, level=None
+):
     for tile in sorted({bond[0] for bond in bonds}):
         rows = slice(8 * tile, 8 * tile + 8)
         own = [motion[axis, layer, rows] for axis in range(3)]
@@ -647,10 +644,13 @@
         near_y = {step_y: own[1] - float(step_y) for step_y in range(-REACH, REACH + 1)}
         force = [total[axis, layer, rows] for axis in range(3)]
         for order, (bond_tile, step_y, step_z, plane, _) in enumerate(bonds):
-            if bond_tile != tile:
+            if bond_tile != tile or level not in (None, step_z == 0):
                 continue
             far_rows = slice(first_row + step_y + 8 * tile, first_row + step_y + 8 * tile + 8)
-            far = [shifts[step_z + REACH, axis, far_layer, far_rows] for axis in range(3)]
+            if level:
+                far = [motion[axis, far_layer, far_rows] for axis in range(3)]
+            else:
+                far = [shifts[step_z + REACH, axis, far_layer, far_rows] for axis in range(3)]
             radial = [far[0] - near_x, far[1] - near_y[step_y], far[2] - own[2]]
             square = radial[0] * radial[0] + radial[1] * radial[1] + radial[2] * radial[2]
             rest = math.sqrt(sum(part * part for part in OFFSETS[plane]))
@@ -660,23 +660,36 @@
             total[axis, layer, rows] = force[axis]
 
 
-def add_inner(extent, late, fill, motion, shifts, weights, total):
-    lax.fori_loop(0, extent[0], fill, 0, unroll=UNROLL_FILL)
+def add_inner(extent, late, motion, shifts, weights, total, level=None):
+    first_row = 0 if level else FIRST
     for step, first, last, bonds, base in inner_plan(extent, late)[0]:
-        if not bonds:
+        if not any(level in (None, bond[2] == 0) for bond in bonds):
             continue
 
         def one_layer(layer, carry, step=step, first=first, bonds=bonds, base=base):
             slot = base + (layer - first) * len(bonds)
-            add_bonds(bonds, step, layer, layer + step, FIRST, motion, shifts, weights, slot, total)
+            add_bonds(
+                bonds, step, layer, layer + step, first_row, motion, shifts, weights, slot, total,
+                level,
+            )
             return carry
 
         lax.fori_loop(first, last, one_layer, 0, unroll=UNROLL if last - first > 1 else 1)
 
 
-def force_early_kernel(extent, edges, motion, z_low, z_high, weights, total, shifts, besides):
-    size_x, size_y, _ = extent
+def force_level_kernel(extent, motion, weights, total):
     total[...] = jnp.zeros(total.shape, jnp.float32)
+    add_inner(extent, False, motion, None, weights, total, True)
+
+
+def force_early_kernel(extent, levelled, edges, motion, z_low, z_high, weights, *refs):
+    size_x, size_y, _ = extent
+    if levelled:
+        level, total, shifts, besides = refs
+        total[...] = level[...]
+    else:
+        total, shifts, besides = refs
+        total[...] = jnp.zeros(total.shape, jnp.float32)
     low_pack = kept(edges[0], z_low[0:size_y])
     high_pack = kept(edges[1], z_high[0:size_y])
     for layer in range(size_x):
@@ -691,7 +704,8 @@
                 shifts[order, axis, layer, FIRST : FIRST + size_y] = value
         return carry
 
-    add_inner(extent, False, fill, motion, shifts, weights, total)
+    lax.fori_loop(0, size_x, fill, 0, unroll=UNROLL_FILL)
+    add_inner(extent, False, motion, shifts, weights, total, False if levelled else None)
 
 
 def force_late_kernel(
@@ -729,7 +743,8 @@
                 shifts[order, axis, layer, above : above + REACH] = value[0:REACH]
         return carry
 
-    add_inner(extent, True, fill, motion, shifts, weights, total)
+    lax.fori_loop(0, size_x, fill, 0, unroll=UNROLL_FILL)
+    add_inner(extent, True, motion, shifts, weights, total)
 
 
 def finish_kernel(
@@ -885,9 +900,10 @@
         ], name="weights_early", far=[broken],
     )
 
-    def force_early(motion, z_low, z_high):
+    def force_early(motion, z_low, z_high, *level):
         return call(
-            part(force_early_kernel, extent), [edges], [motion, z_low, z_high, weights_early],
+            part(force_early_kernel, extent, bool(level)), [edges],
+            [motion, z_low, z_high, weights_early, *level],
             [vector, (moves, 3, size_x, tall, LANES)], [vector], name="force_early",
         )
 
@@ -914,16 +930,16 @@
         ], [(3, size_x, height, LANES)], name="x_layers_first",
     )
     x_near, x_far = swapped(x_near, x_far)
-    (weights_late,) = call(
+    weights_late, pressing = call(
         part(weights_late_kernel, extent), [],
-        [stiffness, wide_static, wide_pack, wide_broken, rows_low, rows_high, keeps],
-        [(late_slots, 8, LANES)],
+        [stiffness, pore, wide_static, wide_pack, wide_broken, rows_low, rows_high, keeps],
+        [(late_slots, 8, LANES), vector],
         [(moves, size_x, height, LANES), (size_x, height, LANES)], name="weights_late",
     )
     inner = force_late(5, motion, early, early_shifts, y_low, y_high)
     outer_weights, pressing = call(
         part(weights_outer_kernel, extent), [edges],
-        [stiffness, pore, wide_static, wide_pack, x_up, x_broken, x_far, x_near],
+        [stiffness, pore, wide_static, wide_pack, x_up, x_broken, x_far, x_near, pressing],
         [(outer_slots, 8, LANES), vector],
         [
             (moves, 1, 2 * REACH, height, LANES),
@@ -953,6 +969,11 @@
     for step_index in range(STEPS):
         z_low = sent(z_up, "gz", 1)
         z_high = sent(z_down, "gz", -1)
+        (level,) = call(
+            part(force_level_kernel, extent), [], [motion, weights_early], [vector],
+            name="force_level",
+        )
+        z_low, z_high, level = lax.optimization_barrier((z_low, z_high, level))
         rows = (round_up(3 * size_x * REACH + 2 * REACH), LANES)
         y_up, y_down = call(
             part(y_rows_kernel, extent), [edges], [motion, z_low, z_high], [rows, rows],
@@ -960,7 +981,7 @@
         )
         y_low = sent(y_up, "gy", 1)
         y_high = sent(y_down, "gy", -1)
-        early, early_shifts = force_early(motion, z_low, z_high)
+        early, early_shifts = force_early(motion, z_low, z_high, level)
         y_low, y_high, early = lax.optimization_barrier((y_low, y_high, early))
         layers = round_up(x_place(3, REACH, size_y) + height)
         x_near, x_far = call(

time: 91.5 us -> 89.3 us (0.976)
  waiting for transfers between devices: 5.12 us -> 3.53 us
    ppermute x15, waiting for transfers between devices: 5.1 us -> 3.43 us  [sent(): lax.ppermute(value, axis, [(i, (i + distance) % count) for i in range(cou...]
    pallas_call x18 -> x20, Pallas kernels: 42.6 us -> 42.5 us  [call(): pl.pallas_call(kernel, out_shape=[jax.ShapeDtypeStruct(shape, jnp.float32...]
  transfers between devices with their start and end apart: 21 -> 21, of which waited for: 5 -> 6; matrix products, arithmetic and copies ran while one was open for 0% -> 0% of each run, Pallas kernels for 35% -> 37%
where the time goes in v2:
time: 89.3 us; the launch traced here: 88.4 us
  Pallas kernels  46.3 us (52%)
  starting transfers between devices  37.6 us (42%)
  waiting for transfers between devices  3.53 us (4%)
  between operations  0.91 us (1%)
    pallas_call x20, Pallas kernels, call(): pl.pallas_call(kernel, out_shape=[jax.ShapeDtypeStruct(shape, jnp.float32...  42.5 us
    ppermute x15, starting transfers between devices, sent(): lax.ppermute(value, axis, [(i, (i + distance) % count) for i in range(cou...  25.1 us
    ppermute x3, starting transfers between devices, swapped(): lax.ppermute(far, 'gx', [(i, (i - side[i]) % count) for i in range(count)])  12.5 us
    pallas_call x1, Pallas kernels, on_device(): pl.pallas_call(part(start_kernel, extent), out_shape=[pltpu.VMEM(shape, k...  3.86 us
    ppermute x15, waiting for transfers between devices, sent(): lax.ppermute(value, axis, [(i, (i + distance) % count) for i in range(cou...  3.43 us
  transfers between devices with their start and end apart: 21, of which 6 were waited for; matrix products, arithmetic and copies ran while one was open for 0% of the time, Pallas kernels for 37%

profile of v2, /device:TPU:71, one launch (start us, length us, event | category | flops | bytes accessed | tf_op | source)
XLA Modules:
  0.0 88.4 jit_solution(5927410208361477268)
XLA Ops:
  0.6 3.9 %start.1 = (f32[3,8,16,128]{3,2,1,0:T(8,128)S(1)}, f32[8,16,128]{2,1,0:T(8,128)S(1)}, f32[8,16,128]{2,1,0:T(8,128)S(1)}, f32[152,128]{1,0:T(8,128)S(1)}, f32[152...) custom-call(f32[8]{0:T(128)} %pressure_in.1, ...), custom_call_target="tpu_custom_call" | custom-call | tf_op jit(solution)/shard_map/start/pallas_call | solution.py:846
  4.5 4.8 %collective-permute-start.4 = (f32[1120,128]{1,0:T(8,128)S(1)}, f32[1120,128]{1,0:T(8,128)S(1)}, u32[]{:S(2)}, u32[]{:S(2)}) collective-permute-start(f32[1120,128]{1,0:T(8,128)S(1)} %get-tuple-element.69.x_up), channel_id=1, source_target_pairs={{0,32},{32,64},{64,96},{96,128},{128,160},{160,192},{192,224},{224... | collective-permute-start | bytes 1720328 | tf_op jit(solution)/shard_map/ppermute | solution.py:813
  9.3 0.7 collective-permute-start.5
  10.3 1.3 %collective-permute-start.1 = (f32[152,128]{1,0:T(8,128)S(1)}, f32[152,128]{1,0:T(8,128)S(1)}, u32[]{:S(2)}, u32[]{:S(2)}) collective-permute-start(f32[152,128]{1,0:T(8,128)S(1)} %get-tuple-element.66), channel_id=1, source_target_pairs={{0,3},{1,0},{2,1},{3,2},{4,7},{5,4},{6,5},{7,6},{8,11},{9,8},{10,9... | collective-permute-start | bytes 233480 | tf_op jit(solution)/shard_map/ppermute | solution.py:813
  11.5 2.8 %collective-permute-start.6 = (f32[224,128]{1,0:T(8,128)S(1)}, f32[224,128]{1,0:T(8,128)S(1)}, u32[]{:S(2)}, u32[]{:S(2)}) collective-permute-start(f32[224,128]{1,0:T(8,128)S(1)} %get-tuple-element.75), channel_id=1, source_target_pairs={{0,28},{4,0},{8,4},{12,8},{16,12},{20,16},{24,20},{28,24},{1,29},{... | collective-permute-start | bytes 344072 | tf_op jit(solution)/shard_map/ppermute | solution.py:813
  15.5 1.8 %collective-permute-start.2 = (f32[176,128]{1,0:T(8,128)S(1)}, f32[176,128]{1,0:T(8,128)S(1)}, u32[]{:S(2)}, u32[]{:S(2)}) collective-permute-start(f32[176,128]{1,0:T(8,128)S(1)} %get-tuple-element.67), channel_id=1, source_target_pairs={{0,4},{4,8},{8,12},{12,16},{16,20},{20,24},{24,28},{28,0},{1,5},{5... | collective-permute-start | bytes 270344 | tf_op jit(solution)/shard_map/ppermute | solution.py:813
  17.3 1.8 %collective-permute-start.3 = (f32[176,128]{1,0:T(8,128)S(1)}, f32[176,128]{1,0:T(8,128)S(1)}, u32[]{:S(2)}, u32[]{:S(2)}) collective-permute-start(f32[176,128]{1,0:T(8,128)S(1)} %get-tuple-element.68), channel_id=1, source_target_pairs={{0,28},{4,0},{8,4},{12,8},{16,12},{20,16},{24,20},{28,24},{1,29},{... | collective-permute-start | bytes 270344 | tf_op jit(solution)/shard_map/ppermute | solution.py:813
  19.1 7.9 %weights_early.1 = (f32[1024,8,128]{2,1,0:T(8,128)S(1)}, f32[648,8,128]{2,1,0:T(8,128)S(1)}) custom-call(s32[7]{0:T(128)S(1)} %stack.55.edges, s32[61,8,16,128]{3,2,1,0:T(8,128)} %broken_in.3, f32[8,16,128]{2,1,0:T(8,128)S(1)} %get-tuple-element.63.stiffness, f32[152,128]{1,0:T(8,128)S(1)} %collective-permute-done.z_low, ...), custom_call_target="tpu_custom_call" | custom-call | tf_op jit(solution)/shard_map/weights_early/pallas_call | solution.py:791
  27.0 4.0 %force_early.3 = (f32[3,8,16,128]{3,2,1,0:T(8,128)S(1)}, f32[7,3,8,32,128]{4,3,2,1,0:T(8,128)S(1)}) custom-call(s32[7]{0:T(128)S(1)} %stack.55.edges, f32[3,8,16,128]{3,2,1,0:T(8,128)S(1)} %get-tuple-element.62.motion, f32[152,128]{1,0:T(8,128)S(1)} %collective-permute-done.z_low, f32[152,128]{1,0:T(8,128)S(1)} %collective-permute-done.1.z_high, ...), custom_call_target="tpu_custom_call" | custom-call | tf_op jit(solution)/shard_map/force_early/pallas_call | solution.py:791
  31.1 0.7 x_layers_first.1
  31.8 3.1 %collective-permute-start.7 = (f32[440,128]{1,0:T(8,128)S(1)}, f32[440,128]{1,0:T(8,128)S(1)}, u32[]{:S(2)}, u32[]{:S(2)}) collective-permute-start(f32[440,128]{1,0:T(8,128)S(1)} %get-tuple-element.79), channel_id=1, source_target_pairs={{0,224},{32,64},{64,32},{96,128},{128,96},{160,192},{192,160},{224... | collective-permute-start | bytes 675848 | tf_op jit(solution)/shard_map/ppermute | solution.py:819
  34.9 3.1 %weights_late.1 = (f32[648,8,128]{2,1,0:T(8,128)S(1)}, f32[3,8,16,128]{3,2,1,0:T(8,128)S(1)}) custom-call(f32[8,16,128]{2,1,0:T(8,128)S(1)} %get-tuple-element.63.stiffness, f32[8,16,128]{2,1,0:T(8,128)S(1)} %get-tuple-element.64.pore, f32[2,8,24,128]{3,2,1,0:T(8,128)S(1)} %get-tuple-element.76.wide, f32[2,24,128]{2,1,0:T(8,128)S(1)} %get-tuple-element.77.wide_pack, ...), custom_call_target="tpu_custom_call" | custom-call | tf_op jit(solution)/shard_map/weights_late/pallas_call | solution.py:791
  37.9 2.9 %force_late.3.inner = f32[3,8,16,128]{3,2,1,0:T(8,128)S(1)} custom-call(s32[7]{0:T(128)S(1)} %stack.55.edges, f32[3,8,16,128]{3,2,1,0:T(8,128)S(1)} %get-tuple-element.62.motion, f32[3,8,16,128]{3,2,1,0:T(8,128)S(1)} %get-tuple-element.85.early, f32[7,3,8,32,128]{4,3,2,1,0:T(8,128)S(1)} %get-tuple-element.86.early_shifts, ...), custom_call_target="tpu_custom_call" | custom-call | tf_op jit(solution)/shard_map/force_late/pallas_call | solution.py:791
  40.9 1.0 %weights_outer.1 = (f32[280,8,128]{2,1,0:T(8,128)S(1)}, f32[3,8,16,128]{3,2,1,0:T(8,128)S(1)}) custom-call(s32[7]{0:T(128)S(1)} %stack.55.edges, f32[8,16,128]{2,1,0:T(8,128)S(1)} %get-tuple-element.63.stiffness, f32[8,16,128]{2,1,0:T(8,128)S(1)} %get-tuple-element.64.pore, f32[2,8,24,128]{3,2,1,0:T(8,128)S(1)} %get-tuple-element.76.wide, ...), custom_call_target="tpu_custom_call" | custom-call | tf_op jit(solution)/shard_map/weights_outer/pallas_call | solution.py:791
  42.0 1.7 %finish_first.1 = (f32[3,8,16,128]{3,2,1,0:T(8,128)S(1)}, f32[3,8,16,128]{3,2,1,0:T(8,128)S(1)}, f32[16,128]{1,0:T(8,128)S(1)}, f32[16,128]{1,0:T(8,128)S(1)}) custom-call(s32[7]{0:T(128)S(1)} %stack.55.edges, f32[3,8,16,128]{3,2,1,0:T(8,128)S(1)} %get-tuple-element.62.motion, f32[3,8,16,128]{3,2,1,0:T(8,128)S(1)} %copy-done, ...), custom_call_target="tpu_custom_call" | custom-call | tf_op jit(solution)/shard_map/finish_first/pallas_call | solution.py:791
  43.9 1.5 %collective-permute-start.10 = (f32[16,128]{1,0:T(8,128)S(1)}, f32[16,128]{1,0:T(8,128)S(1)}, u32[]{:S(2)}, u32[]{:S(2)}) collective-permute-start(f32[16,128]{1,0:T(8,128)S(1)} %get-tuple-element.92), channel_id=1, source_target_pairs={{0,3},{1,0},{2,1},{3,2},{4,7},{5,4},{6,5},{7,6},{8,11},{9,8},{10,9... | collective-permute-start | bytes 24584 | tf_op jit(solution)/shard_map/ppermute | solution.py:813
  45.4 0.8 force_level.2.refs_0_
  46.4 1.3 %collective-permute-done.10.z_high = f32[16,128]{1,0:T(8,128)S(1)} collective-permute-done((f32[16,128]{1,0:T(8,128)S(1)}, f32[16,128]{1,0:T(8,128)S(1)}, u32[]{:S(2)}, u32[]{:S(2)}) %collective-permute-start.10) | collective-permute-done | bytes 8224 | tf_op jit(solution)/shard_map/ppermute | solution.py:813
  48.3 2.4 %collective-permute-start.11 = (f32[80,128]{1,0:T(8,128)S(1)}, f32[80,128]{1,0:T(8,128)S(1)}, u32[]{:S(2)}, u32[]{:S(2)}) collective-permute-start(f32[80,128]{1,0:T(8,128)S(1)} %get-tuple-element.95), channel_id=1, source_target_pairs={{0,4},{4,8},{8,12},{12,16},{16,20},{20,24},{24,28},{28,0},{1,5},{5... | collective-permute-start | bytes 122888 | tf_op jit(solution)/shard_map/ppermute | solution.py:813
  50.7 2.2 %collective-permute-start.12 = (f32[80,128]{1,0:T(8,128)S(1)}, f32[80,128]{1,0:T(8,128)S(1)}, u32[]{:S(2)}, u32[]{:S(2)}) collective-permute-start(f32[80,128]{1,0:T(8,128)S(1)} %get-tuple-element.96), channel_id=1, source_target_pairs={{0,28},{4,0},{8,4},{12,8},{16,12},{20,16},{24,20},{28,24},{1,29},{... | collective-permute-start | bytes 122888 | tf_op jit(solution)/shard_map/ppermute | solution.py:813
  53.0 3.3 %force_early.4 = (f32[3,8,16,128]{3,2,1,0:T(8,128)S(1)}, f32[7,3,8,32,128]{4,3,2,1,0:T(8,128)S(1)}) custom-call(s32[7]{0:T(128)S(1)} %stack.55.edges, f32[3,8,16,128]{3,2,1,0:T(8,128)S(1)} %get-tuple-element.89.motion, f32[16,128]{1,0:T(8,128)S(1)} %collective-permute-done.9.z_low, f32[16,128]{1,0:T(8,128)S(1)} %collective-permute-done.10.z_high, ...), custom_call_target="tpu_custom_call" | custom-call | tf_op jit(solution)/shard_map/force_early/pallas_call | solution.py:791
  56.9 4.3 %collective-permute-start.13 = (f32[192,128]{1,0:T(8,128)S(1)}, f32[192,128]{1,0:T(8,128)S(1)}, u32[]{:S(2)}, u32[]{:S(2)}) collective-permute-start(f32[192,128]{1,0:T(8,128)S(1)} %get-tuple-element.103), channel_id=1, source_target_pairs={{0,224},{32,64},{64,32},{96,128},{128,96},{160,192},{192,160},{224... | collective-permute-start | bytes 294920 | tf_op jit(solution)/shard_map/ppermute | solution.py:819
  61.2 2.9 %force_late.4.inner = f32[3,8,16,128]{3,2,1,0:T(8,128)S(1)} custom-call(s32[7]{0:T(128)S(1)} %stack.55.edges, f32[3,8,16,128]{3,2,1,0:T(8,128)S(1)} %get-tuple-element.89.motion, f32[3,8,16,128]{3,2,1,0:T(8,128)S(1)} %get-tuple-element.99.early, f32[7,3,8,32,128]{4,3,2,1,0:T(8,128)S(1)} %get-tuple-element.100.early_shifts, ...), custom_call_target="tpu_custom_call" | custom-call | tf_op jit(solution)/shard_map/force_late/pallas_call | solution.py:791
  64.2 1.7 %finish_middle.1 = (f32[3,8,16,128]{3,2,1,0:T(8,128)S(1)}, f32[3,8,16,128]{3,2,1,0:T(8,128)S(1)}, f32[16,128]{1,0:T(8,128)S(1)}, f32[16,128]{1,0:T(8,128)S(1)}) custom-call(s32[7]{0:T(128)S(1)} %stack.55.edges, f32[3,8,16,128]{3,2,1,0:T(8,128)S(1)} %get-tuple-element.89.motion, f32[3,8,16,128]{3,2,1,0:T(8,128)S(1)} %get-tuple-element.90.speed, ...), custom_call_target="tpu_custom_call" | custom-call | tf_op jit(solution)/shard_map/finish_middle/pallas_call | solution.py:791
  66.0 1.5 %collective-permute-start.16 = (f32[16,128]{1,0:T(8,128)S(1)}, f32[16,128]{1,0:T(8,128)S(1)}, u32[]{:S(2)}, u32[]{:S(2)}) collective-permute-start(f32[16,128]{1,0:T(8,128)S(1)} %get-tuple-element.108), channel_id=1, source_target_pairs={{0,3},{1,0},{2,1},{3,2},{4,7},{5,4},{6,5},{7,6},{8,11},{9,8},{10,9... | collective-permute-start | bytes 24584 | tf_op jit(solution)/shard_map/ppermute | solution.py:813
  67.4 0.8 force_level.3.refs_0_
  68.5 1.3 %collective-permute-done.16.z_high = f32[16,128]{1,0:T(8,128)S(1)} collective-permute-done((f32[16,128]{1,0:T(8,128)S(1)}, f32[16,128]{1,0:T(8,128)S(1)}, u32[]{:S(2)}, u32[]{:S(2)}) %collective-permute-start.16) | collective-permute-done | bytes 8224 | tf_op jit(solution)/shard_map/ppermute | solution.py:813
  70.4 3.6 %collective-permute-start.18 = (f32[80,128]{1,0:T(8,128)S(1)}, f32[80,128]{1,0:T(8,128)S(1)}, u32[]{:S(2)}, u32[]{:S(2)}) collective-permute-start(f32[80,128]{1,0:T(8,128)S(1)} %get-tuple-element.112), channel_id=1, source_target_pairs={{0,28},{4,0},{8,4},{12,8},{16,12},{20,16},{24,20},{28,24},{1,29},{... | collective-permute-start | bytes 122888 | tf_op jit(solution)/shard_map/ppermute | solution.py:813
  74.0 3.3 %force_early.5 = (f32[3,8,16,128]{3,2,1,0:T(8,128)S(1)}, f32[7,3,8,32,128]{4,3,2,1,0:T(8,128)S(1)}) custom-call(s32[7]{0:T(128)S(1)} %stack.55.edges, f32[3,8,16,128]{3,2,1,0:T(8,128)S(1)} %get-tuple-element.105.motion, f32[16,128]{1,0:T(8,128)S(1)} %collective-permute-done.15.z_low, f32[16,128]{1,0:T(8,128)S(1)} %collective-permute-done.16.z_high, ...), custom_call_target="tpu_custom_call" | custom-call | tf_op jit(solution)/shard_map/force_early/pallas_call | solution.py:791
  78.0 5.1 %collective-permute-start.19 = (f32[192,128]{1,0:T(8,128)S(1)}, f32[192,128]{1,0:T(8,128)S(1)}, u32[]{:S(2)}, u32[]{:S(2)}) collective-permute-start(f32[192,128]{1,0:T(8,128)S(1)} %get-tuple-element.119), channel_id=1, source_target_pairs={{0,224},{32,64},{64,32},{96,128},{128,96},{160,192},{192,160},{224... | collective-permute-start | bytes 294920 | tf_op jit(solution)/shard_map/ppermute | solution.py:819
  83.1 2.9 %force_late.5.inner = f32[3,8,16,128]{3,2,1,0:T(8,128)S(1)} custom-call(s32[7]{0:T(128)S(1)} %stack.55.edges, f32[3,8,16,128]{3,2,1,0:T(8,128)S(1)} %get-tuple-element.105.motion, f32[3,8,16,128]{3,2,1,0:T(8,128)S(1)} %get-tuple-element.115.early, f32[7,3,8,32,128]{4,3,2,1,0:T(8,128)S(1)} %get-tuple-element.116.early_shifts, ...), custom_call_target="tpu_custom_call" | custom-call | tf_op jit(solution)/shard_map/force_late/pallas_call | solution.py:791
  86.1 2.3 %finish_last.1 = (f32[3,8,16,128]{3,2,1,0:T(8,128)}, f32[3,8,16,128]{3,2,1,0:T(8,128)}, f32[3,8,16,128]{3,2,1,0:T(8,128)}) custom-call(s32[7]{0:T(128)S(1)} %stack.55.edges, f32[3,8,16,128]{3,2,1,0:T(8,128)S(1)} %get-tuple-element.105.motion, f32[3,8,16,128]{3,2,1,0:T(8,128)S(1)} %get-tuple-element.106.speed, ...), custom_call_target="tpu_custom_call" | custom-call | tf_op jit(solution)/shard_map/finish_last/pallas_call | solution.py:791
  (34 shorter events, 4.7 us)
Async XLA Ops:
  4.5 26.6 %collective-permute-start.4 = (f32[1120,128]{1,0:T(8,128)S(1)}, f32[1120,128]{1,0:T(8,128)S(1)}, u32[]{:S(2)}, u32[]{:S(2)}) collective-permute-start(f32[1120,128]{1,0:T(8,128)S(1)} %get-tuple-element.69.x_up), channel_id=1, source_target_pairs={{0,32},{32,64},{64,96},{96,128},{128,160},{160,192},{192,224},{224... | collective-permute-start | bytes 1720328 | tf_op jit(solution)/shard_map/ppermute | solution.py:813
  9.3 21.7 %collective-permute-start.5 = (f32[368,128]{1,0:T(8,128)S(1)}, f32[368,128]{1,0:T(8,128)S(1)}, u32[]{:S(2)}, u32[]{:S(2)}) collective-permute-start(f32[368,128]{1,0:T(8,128)S(1)} %get-tuple-element.74), channel_id=1, source_target_pairs={{0,4},{4,8},{8,12},{12,16},{16,20},{20,24},{24,28},{28,0},{1,5},{5... | collective-permute-start | bytes 565256 | tf_op jit(solution)/shard_map/ppermute | solution.py:813
  10.1 4.4 %collective-permute-start = (f32[152,128]{1,0:T(8,128)S(1)}, f32[152,128]{1,0:T(8,128)S(1)}, u32[]{:S(2)}, u32[]{:S(2)}) collective-permute-start(f32[152,128]{1,0:T(8,128)S(1)} %get-tuple-element.65), channel_id=1, source_target_pairs={{0,1},{1,2},{2,3},{3,0},{4,5},{5,6},{6,7},{7,4},{8,9},{9,10},{10,1... | collective-permute-start | bytes 233480 | tf_op jit(solution)/shard_map/ppermute | solution.py:813
  10.3 4.6 %collective-permute-start.1 = (f32[152,128]{1,0:T(8,128)S(1)}, f32[152,128]{1,0:T(8,128)S(1)}, u32[]{:S(2)}, u32[]{:S(2)}) collective-permute-start(f32[152,128]{1,0:T(8,128)S(1)} %get-tuple-element.66), channel_id=1, source_target_pairs={{0,3},{1,0},{2,1},{3,2},{4,7},{5,4},{6,5},{7,6},{8,11},{9,8},{10,9... | collective-permute-start | bytes 233480 | tf_op jit(solution)/shard_map/ppermute | solution.py:813
  11.5 19.5 %collective-permute-start.6 = (f32[224,128]{1,0:T(8,128)S(1)}, f32[224,128]{1,0:T(8,128)S(1)}, u32[]{:S(2)}, u32[]{:S(2)}) collective-permute-start(f32[224,128]{1,0:T(8,128)S(1)} %get-tuple-element.75), channel_id=1, source_target_pairs={{0,28},{4,0},{8,4},{12,8},{16,12},{20,16},{24,20},{28,24},{1,29},{... | collective-permute-start | bytes 344072 | tf_op jit(solution)/shard_map/ppermute | solution.py:813
  15.5 15.6 %collective-permute-start.2 = (f32[176,128]{1,0:T(8,128)S(1)}, f32[176,128]{1,0:T(8,128)S(1)}, u32[]{:S(2)}, u32[]{:S(2)}) collective-permute-start(f32[176,128]{1,0:T(8,128)S(1)} %get-tuple-element.67), channel_id=1, source_target_pairs={{0,4},{4,8},{8,12},{12,16},{16,20},{20,24},{24,28},{28,0},{1,5},{5... | collective-permute-start | bytes 270344 | tf_op jit(solution)/shard_map/ppermute | solution.py:813
  17.3 13.8 %collective-permute-start.3 = (f32[176,128]{1,0:T(8,128)S(1)}, f32[176,128]{1,0:T(8,128)S(1)}, u32[]{:S(2)}, u32[]{:S(2)}) collective-permute-start(f32[176,128]{1,0:T(8,128)S(1)} %get-tuple-element.68), channel_id=1, source_target_pairs={{0,28},{4,0},{8,4},{12,8},{16,12},{20,16},{24,20},{28,24},{1,29},{... | collective-permute-start | bytes 270344 | tf_op jit(solution)/shard_map/ppermute | solution.py:813
  31.8 9.1 %collective-permute-start.7 = (f32[440,128]{1,0:T(8,128)S(1)}, f32[440,128]{1,0:T(8,128)S(1)}, u32[]{:S(2)}, u32[]{:S(2)}) collective-permute-start(f32[440,128]{1,0:T(8,128)S(1)} %get-tuple-element.79), channel_id=1, source_target_pairs={{0,224},{32,64},{64,32},{96,128},{128,96},{160,192},{192,160},{224... | collective-permute-start | bytes 675848 | tf_op jit(solution)/shard_map/ppermute | solution.py:819
  34.9 6.0 %collective-permute-start.8 = (f32[440,128]{1,0:T(8,128)S(1)}, f32[440,128]{1,0:T(8,128)S(1)}, u32[]{:S(2)}, u32[]{:S(2)}) collective-permute-start(f32[440,128]{1,0:T(8,128)S(1)} %get-tuple-element.80), channel_id=1, source_target_pairs={{0,32},{32,0},{64,96},{96,64},{128,160},{160,128},{192,224},{224,1... | collective-permute-start | bytes 675848 | tf_op jit(solution)/shard_map/ppermute | solution.py:820
  37.9 4.0 %copy-start = (f32[3,8,16,128]{3,2,1,0:T(8,128)S(1)}, f32[3,8,16,128]{3,2,1,0:T(8,128)}, u32[]{:S(2)}) copy-start(f32[3,8,16,128]{3,2,1,0:T(8,128)} %speed.1) | copy-start | bytes 589828
  43.7 2.8 %collective-permute-start.9 = (f32[16,128]{1,0:T(8,128)S(1)}, f32[16,128]{1,0:T(8,128)S(1)}, u32[]{:S(2)}, u32[]{:S(2)}) collective-permute-start(f32[16,128]{1,0:T(8,128)S(1)} %get-tuple-element.91), channel_id=1, source_target_pairs={{0,1},{1,2},{2,3},{3,0},{4,5},{5,6},{6,7},{7,4},{8,9},{9,10},{10,1... | collective-permute-start | bytes 24584 | tf_op jit(solution)/shard_map/ppermute | solution.py:813
  43.9 3.8 %collective-permute-start.10 = (f32[16,128]{1,0:T(8,128)S(1)}, f32[16,128]{1,0:T(8,128)S(1)}, u32[]{:S(2)}, u32[]{:S(2)}) collective-permute-start(f32[16,128]{1,0:T(8,128)S(1)} %get-tuple-element.92), channel_id=1, source_target_pairs={{0,3},{1,0},{2,1},{3,2},{4,7},{5,4},{6,5},{7,6},{8,11},{9,8},{10,9... | collective-permute-start | bytes 24584 | tf_op jit(solution)/shard_map/ppermute | solution.py:813
  48.3 8.0 %collective-permute-start.11 = (f32[80,128]{1,0:T(8,128)S(1)}, f32[80,128]{1,0:T(8,128)S(1)}, u32[]{:S(2)}, u32[]{:S(2)}) collective-permute-start(f32[80,128]{1,0:T(8,128)S(1)} %get-tuple-element.95), channel_id=1, source_target_pairs={{0,4},{4,8},{8,12},{12,16},{16,20},{20,24},{24,28},{28,0},{1,5},{5... | collective-permute-start | bytes 122888 | tf_op jit(solution)/shard_map/ppermute | solution.py:813
  50.7 5.5 %collective-permute-start.12 = (f32[80,128]{1,0:T(8,128)S(1)}, f32[80,128]{1,0:T(8,128)S(1)}, u32[]{:S(2)}, u32[]{:S(2)}) collective-permute-start(f32[80,128]{1,0:T(8,128)S(1)} %get-tuple-element.96), channel_id=1, source_target_pairs={{0,28},{4,0},{8,4},{12,8},{16,12},{20,16},{24,20},{28,24},{1,29},{... | collective-permute-start | bytes 122888 | tf_op jit(solution)/shard_map/ppermute | solution.py:813
  56.9 7.2 %collective-permute-start.13 = (f32[192,128]{1,0:T(8,128)S(1)}, f32[192,128]{1,0:T(8,128)S(1)}, u32[]{:S(2)}, u32[]{:S(2)}) collective-permute-start(f32[192,128]{1,0:T(8,128)S(1)} %get-tuple-element.103), channel_id=1, source_target_pairs={{0,224},{32,64},{64,32},{96,128},{128,96},{160,192},{192,160},{224... | collective-permute-start | bytes 294920 | tf_op jit(solution)/shard_map/ppermute | solution.py:819
  61.2 3.0 %collective-permute-start.14 = (f32[192,128]{1,0:T(8,128)S(1)}, f32[192,128]{1,0:T(8,128)S(1)}, u32[]{:S(2)}, u32[]{:S(2)}) collective-permute-start(f32[192,128]{1,0:T(8,128)S(1)} %get-tuple-element.104), channel_id=1, source_target_pairs={{0,32},{32,0},{64,96},{96,64},{128,160},{160,128},{192,224},{224,1... | collective-permute-start | bytes 294920 | tf_op jit(solution)/shard_map/ppermute | solution.py:820
  65.9 2.6 %collective-permute-start.15 = (f32[16,128]{1,0:T(8,128)S(1)}, f32[16,128]{1,0:T(8,128)S(1)}, u32[]{:S(2)}, u32[]{:S(2)}) collective-permute-start(f32[16,128]{1,0:T(8,128)S(1)} %get-tuple-element.107), channel_id=1, source_target_pairs={{0,1},{1,2},{2,3},{3,0},{4,5},{5,6},{6,7},{7,4},{8,9},{9,10},{10,1... | collective-permute-start | bytes 24584 | tf_op jit(solution)/shard_map/ppermute | solution.py:813
  66.0 3.8 %collective-permute-start.16 = (f32[16,128]{1,0:T(8,128)S(1)}, f32[16,128]{1,0:T(8,128)S(1)}, u32[]{:S(2)}, u32[]{:S(2)}) collective-permute-start(f32[16,128]{1,0:T(8,128)S(1)} %get-tuple-element.108), channel_id=1, source_target_pairs={{0,3},{1,0},{2,1},{3,2},{4,7},{5,4},{6,5},{7,6},{8,11},{9,8},{10,9... | collective-permute-start | bytes 24584 | tf_op jit(solution)/shard_map/ppermute | solution.py:813
  70.3 7.0 %collective-permute-start.17 = (f32[80,128]{1,0:T(8,128)S(1)}, f32[80,128]{1,0:T(8,128)S(1)}, u32[]{:S(2)}, u32[]{:S(2)}) collective-permute-start(f32[80,128]{1,0:T(8,128)S(1)} %get-tuple-element.111), channel_id=1, source_target_pairs={{0,4},{4,8},{8,12},{12,16},{16,20},{20,24},{24,28},{28,0},{1,5},{5... | collective-permute-start | bytes 122888 | tf_op jit(solution)/shard_map/ppermute | solution.py:813
  70.4 6.9 %collective-permute-start.18 = (f32[80,128]{1,0:T(8,128)S(1)}, f32[80,128]{1,0:T(8,128)S(1)}, u32[]{:S(2)}, u32[]{:S(2)}) collective-permute-start(f32[80,128]{1,0:T(8,128)S(1)} %get-tuple-element.112), channel_id=1, source_target_pairs={{0,28},{4,0},{8,4},{12,8},{16,12},{20,16},{24,20},{28,24},{1,29},{... | collective-permute-start | bytes 122888 | tf_op jit(solution)/shard_map/ppermute | solution.py:813
  78.0 8.1 %collective-permute-start.19 = (f32[192,128]{1,0:T(8,128)S(1)}, f32[192,128]{1,0:T(8,128)S(1)}, u32[]{:S(2)}, u32[]{:S(2)}) collective-permute-start(f32[192,128]{1,0:T(8,128)S(1)} %get-tuple-element.119), channel_id=1, source_target_pairs={{0,224},{32,64},{64,32},{96,128},{128,96},{160,192},{192,160},{224... | collective-permute-start | bytes 294920 | tf_op jit(solution)/shard_map/ppermute | solution.py:819
  83.1 3.0 %collective-permute-start.20 = (f32[192,128]{1,0:T(8,128)S(1)}, f32[192,128]{1,0:T(8,128)S(1)}, u32[]{:S(2)}, u32[]{:S(2)}) collective-permute-start(f32[192,128]{1,0:T(8,128)S(1)} %get-tuple-element.120), channel_id=1, source_target_pairs={{0,32},{32,0},{64,96},{96,64},{128,160},{160,128},{192,224},{224,1... | collective-permute-start | bytes 294920 | tf_op jit(solution)/shard_map/ppermute | solution.py:820

commit v3 on v2

--- a/solution.py
+++ b/solution.py
@@ -509,7 +509,7 @@
                     target[slot + order] = keep
                 return carry
 
-            lax.fori_loop(first, last, one_layer, 0)
+            lax.fori_loop(first, last, one_layer, 0, unroll=UNROLL if last - first > 1 else 1)
 
 
 def pressed(inside, level, own, sign):
@@ -576,7 +576,7 @@
                 )
             return carry
 
-        lax.fori_loop(first, last, one_layer, 0)
+        lax.fori_loop(first, last, one_layer, 0, unroll=UNROLL if last - first > 1 else 1)
 
 
 def weights_outer_kernel(

time: 89.3 us -> 88.3 us (0.989)
  Pallas kernels: 46.3 us -> 44 us
  waiting for transfers between devices: 3.53 us -> 5.4 us
    ppermute x3, starting transfers between devices: 12.5 us -> 10.1 us  [swapped(): lax.ppermute(far, 'gx', [(i, (i - side[i]) % count) for i in range(count)])]
    pallas_call x20, Pallas kernels: 42.5 us -> 40.1 us  [call(): pl.pallas_call(kernel, out_shape=[jax.ShapeDtypeStruct(shape, jnp.float32...]
    ppermute x15, starting transfers between devices: 25.1 us -> 26.8 us  [sent(): lax.ppermute(value, axis, [(i, (i + distance) % count) for i in range(cou...]
    ppermute x15, waiting for transfers between devices: 3.43 us -> 4.87 us  [sent(): lax.ppermute(value, axis, [(i, (i + distance) % count) for i in range(cou...]
  transfers between devices with their start and end apart: 21 -> 21, of which waited for: 6 -> 9; matrix products, arithmetic and copies ran while one was open for 0% -> 0% of each run, Pallas kernels for 37% -> 35%
where the time goes in v3:
time: 88.3 us; the launch traced here: 87.2 us
  Pallas kernels  44 us (50%)
  starting transfers between devices  36.9 us (42%)
  waiting for transfers between devices  5.4 us (6%)
    pallas_call x20, Pallas kernels, call(): pl.pallas_call(kernel, out_shape=[jax.ShapeDtypeStruct(shape, jnp.float32...  40.1 us
    ppermute x15, starting transfers between devices, sent(): lax.ppermute(value, axis, [(i, (i + distance) % count) for i in range(cou...  26.8 us
    ppermute x3, starting transfers between devices, swapped(): lax.ppermute(far, 'gx', [(i, (i - side[i]) % count) for i in range(count)])  10.1 us
    ppermute x15, waiting for transfers between devices, sent(): lax.ppermute(value, axis, [(i, (i + distance) % count) for i in range(cou...  4.87 us
    pallas_call x1, Pallas kernels, on_device(): pl.pallas_call(part(start_kernel, extent), out_shape=[pltpu.VMEM(shape, k...  3.86 us
  transfers between devices with their start and end apart: 21, of which 9 were waited for; matrix products, arithmetic and copies ran while one was open for 0% of the time, Pallas kernels for 35%

profile of v3, /device:TPU:71, one launch (start us, length us, event | category | flops | bytes accessed | tf_op | source)
XLA Modules:
  0.0 87.2 jit_solution(1347011673365193462)
XLA Ops:
  0.6 3.9 %start.1 = (f32[3,8,16,128]{3,2,1,0:T(8,128)S(1)}, f32[8,16,128]{2,1,0:T(8,128)S(1)}, f32[8,16,128]{2,1,0:T(8,128)S(1)}, f32[152,128]{1,0:T(8,128)S(1)}, f32[152...) custom-call(f32[8]{0:T(128)} %pressure_in.1, ...), custom_call_target="tpu_custom_call" | custom-call | tf_op jit(solution)/shard_map/start/pallas_call | solution.py:846
  4.5 4.8 %collective-permute-start.4 = (f32[1120,128]{1,0:T(8,128)S(1)}, f32[1120,128]{1,0:T(8,128)S(1)}, u32[]{:S(2)}, u32[]{:S(2)}) collective-permute-start(f32[1120,128]{1,0:T(8,128)S(1)} %get-tuple-element.69.x_up), channel_id=1, source_target_pairs={{0,32},{32,64},{64,96},{96,128},{128,160},{160,192},{192,224},{224... | collective-permute-start | bytes 1720328 | tf_op jit(solution)/shard_map/ppermute | solution.py:813
  9.3 0.7 collective-permute-start.5
  10.3 1.3 %collective-permute-start.1 = (f32[152,128]{1,0:T(8,128)S(1)}, f32[152,128]{1,0:T(8,128)S(1)}, u32[]{:S(2)}, u32[]{:S(2)}) collective-permute-start(f32[152,128]{1,0:T(8,128)S(1)} %get-tuple-element.66), channel_id=1, source_target_pairs={{0,3},{1,0},{2,1},{3,2},{4,7},{5,4},{6,5},{7,6},{8,11},{9,8},{10,9... | collective-permute-start | bytes 233480 | tf_op jit(solution)/shard_map/ppermute | solution.py:813
  11.5 2.8 %collective-permute-start.6 = (f32[224,128]{1,0:T(8,128)S(1)}, f32[224,128]{1,0:T(8,128)S(1)}, u32[]{:S(2)}, u32[]{:S(2)}) collective-permute-start(f32[224,128]{1,0:T(8,128)S(1)} %get-tuple-element.75), channel_id=1, source_target_pairs={{0,28},{4,0},{8,4},{12,8},{16,12},{20,16},{24,20},{28,24},{1,29},{... | collective-permute-start | bytes 344072 | tf_op jit(solution)/shard_map/ppermute | solution.py:813
  15.5 1.8 %collective-permute-start.2 = (f32[176,128]{1,0:T(8,128)S(1)}, f32[176,128]{1,0:T(8,128)S(1)}, u32[]{:S(2)}, u32[]{:S(2)}) collective-permute-start(f32[176,128]{1,0:T(8,128)S(1)} %get-tuple-element.67), channel_id=1, source_target_pairs={{0,4},{4,8},{8,12},{12,16},{16,20},{20,24},{24,28},{28,0},{1,5},{5... | collective-permute-start | bytes 270344 | tf_op jit(solution)/shard_map/ppermute | solution.py:813
  17.3 1.8 %collective-permute-start.3 = (f32[176,128]{1,0:T(8,128)S(1)}, f32[176,128]{1,0:T(8,128)S(1)}, u32[]{:S(2)}, u32[]{:S(2)}) collective-permute-start(f32[176,128]{1,0:T(8,128)S(1)} %get-tuple-element.68), channel_id=1, source_target_pairs={{0,28},{4,0},{8,4},{12,8},{16,12},{20,16},{24,20},{28,24},{1,29},{... | collective-permute-start | bytes 270344 | tf_op jit(solution)/shard_map/ppermute | solution.py:813
  19.1 6.3 %weights_early.1 = (f32[1024,8,128]{2,1,0:T(8,128)S(1)}, f32[648,8,128]{2,1,0:T(8,128)S(1)}) custom-call(s32[7]{0:T(128)S(1)} %stack.55.edges, s32[61,8,16,128]{3,2,1,0:T(8,128)} %broken_in.3, f32[8,16,128]{2,1,0:T(8,128)S(1)} %get-tuple-element.63.stiffness, f32[152,128]{1,0:T(8,128)S(1)} %collective-permute-done.z_low, ...), custom_call_target="tpu_custom_call" | custom-call | tf_op jit(solution)/shard_map/weights_early/pallas_call | solution.py:791
  25.5 4.0 %force_early.3 = (f32[3,8,16,128]{3,2,1,0:T(8,128)S(1)}, f32[7,3,8,32,128]{4,3,2,1,0:T(8,128)S(1)}) custom-call(s32[7]{0:T(128)S(1)} %stack.55.edges, f32[3,8,16,128]{3,2,1,0:T(8,128)S(1)} %get-tuple-element.62.motion, f32[152,128]{1,0:T(8,128)S(1)} %collective-permute-done.z_low, f32[152,128]{1,0:T(8,128)S(1)} %collective-permute-done.1.z_high, ...), custom_call_target="tpu_custom_call" | custom-call | tf_op jit(solution)/shard_map/force_early/pallas_call | solution.py:791
  29.6 1.0 %collective-permute-done.3.y_high = f32[176,128]{1,0:T(8,128)S(1)} collective-permute-done((f32[176,128]{1,0:T(8,128)S(1)}, f32[176,128]{1,0:T(8,128)S(1)}, u32[]{:S(2)}, u32[]{:S(2)}) %collective-permute-start.3) | collective-permute-done | bytes 90144 | tf_op jit(solution)/shard_map/ppermute | solution.py:813
  31.3 2.0 %collective-permute-start.7 = (f32[440,128]{1,0:T(8,128)S(1)}, f32[440,128]{1,0:T(8,128)S(1)}, u32[]{:S(2)}, u32[]{:S(2)}) collective-permute-start(f32[440,128]{1,0:T(8,128)S(1)} %get-tuple-element.79), channel_id=1, source_target_pairs={{0,224},{32,64},{64,32},{96,128},{128,96},{160,192},{192,160},{224... | collective-permute-start | bytes 675848 | tf_op jit(solution)/shard_map/ppermute | solution.py:819
  33.3 2.3 %weights_late.1 = (f32[648,8,128]{2,1,0:T(8,128)S(1)}, f32[3,8,16,128]{3,2,1,0:T(8,128)S(1)}) custom-call(f32[8,16,128]{2,1,0:T(8,128)S(1)} %get-tuple-element.63.stiffness, f32[8,16,128]{2,1,0:T(8,128)S(1)} %get-tuple-element.64.pore, f32[2,8,24,128]{3,2,1,0:T(8,128)S(1)} %get-tuple-element.76.wide, f32[2,24,128]{2,1,0:T(8,128)S(1)} %get-tuple-element.77.wide_pack, ...), custom_call_target="tpu_custom_call" | custom-call | tf_op jit(solution)/shard_map/weights_late/pallas_call | solution.py:791
  35.6 2.9 %force_late.3.inner = f32[3,8,16,128]{3,2,1,0:T(8,128)S(1)} custom-call(s32[7]{0:T(128)S(1)} %stack.55.edges, f32[3,8,16,128]{3,2,1,0:T(8,128)S(1)} %get-tuple-element.62.motion, f32[3,8,16,128]{3,2,1,0:T(8,128)S(1)} %get-tuple-element.85.early, f32[7,3,8,32,128]{4,3,2,1,0:T(8,128)S(1)} %get-tuple-element.86.early_shifts, ...), custom_call_target="tpu_custom_call" | custom-call | tf_op jit(solution)/shard_map/force_late/pallas_call | solution.py:791
  39.0 1.0 %weights_outer.1 = (f32[280,8,128]{2,1,0:T(8,128)S(1)}, f32[3,8,16,128]{3,2,1,0:T(8,128)S(1)}) custom-call(s32[7]{0:T(128)S(1)} %stack.55.edges, f32[8,16,128]{2,1,0:T(8,128)S(1)} %get-tuple-element.63.stiffness, f32[8,16,128]{2,1,0:T(8,128)S(1)} %get-tuple-element.64.pore, f32[2,8,24,128]{3,2,1,0:T(8,128)S(1)} %get-tuple-element.76.wide, ...), custom_call_target="tpu_custom_call" | custom-call | tf_op jit(solution)/shard_map/weights_outer/pallas_call | solution.py:791
  40.0 1.7 %finish_first.1 = (f32[3,8,16,128]{3,2,1,0:T(8,128)S(1)}, f32[3,8,16,128]{3,2,1,0:T(8,128)S(1)}, f32[16,128]{1,0:T(8,128)S(1)}, f32[16,128]{1,0:T(8,128)S(1)}) custom-call(s32[7]{0:T(128)S(1)} %stack.55.edges, f32[3,8,16,128]{3,2,1,0:T(8,128)S(1)} %get-tuple-element.62.motion, f32[3,8,16,128]{3,2,1,0:T(8,128)S(1)} %copy-done, ...), custom_call_target="tpu_custom_call" | custom-call | tf_op jit(solution)/shard_map/finish_first/pallas_call | solution.py:791
  42.0 1.3 %collective-permute-start.10 = (f32[16,128]{1,0:T(8,128)S(1)}, f32[16,128]{1,0:T(8,128)S(1)}, u32[]{:S(2)}, u32[]{:S(2)}) collective-permute-start(f32[16,128]{1,0:T(8,128)S(1)} %get-tuple-element.92), channel_id=1, source_target_pairs={{0,3},{1,0},{2,1},{3,2},{4,7},{5,4},{6,5},{7,6},{8,11},{9,8},{10,9... | collective-permute-start | bytes 24584 | tf_op jit(solution)/shard_map/ppermute | solution.py:813
  43.3 0.8 force_level.2.refs_0_
  44.3 1.4 %collective-permute-done.10.z_high = f32[16,128]{1,0:T(8,128)S(1)} collective-permute-done((f32[16,128]{1,0:T(8,128)S(1)}, f32[16,128]{1,0:T(8,128)S(1)}, u32[]{:S(2)}, u32[]{:S(2)}) %collective-permute-start.10) | collective-permute-done | bytes 8224 | tf_op jit(solution)/shard_map/ppermute | solution.py:813
  46.3 4.3 %collective-permute-start.11 = (f32[80,128]{1,0:T(8,128)S(1)}, f32[80,128]{1,0:T(8,128)S(1)}, u32[]{:S(2)}, u32[]{:S(2)}) collective-permute-start(f32[80,128]{1,0:T(8,128)S(1)} %get-tuple-element.95), channel_id=1, source_target_pairs={{0,4},{4,8},{8,12},{12,16},{16,20},{20,24},{24,28},{28,0},{1,5},{5... | collective-permute-start | bytes 122888 | tf_op jit(solution)/shard_map/ppermute | solution.py:813
  50.6 2.2 %collective-permute-start.12 = (f32[80,128]{1,0:T(8,128)S(1)}, f32[80,128]{1,0:T(8,128)S(1)}, u32[]{:S(2)}, u32[]{:S(2)}) collective-permute-start(f32[80,128]{1,0:T(8,128)S(1)} %get-tuple-element.96), channel_id=1, source_target_pairs={{0,28},{4,0},{8,4},{12,8},{16,12},{20,16},{24,20},{28,24},{1,29},{... | collective-permute-start | bytes 122888 | tf_op jit(solution)/shard_map/ppermute | solution.py:813
  52.8 3.3 %force_early.4 = (f32[3,8,16,128]{3,2,1,0:T(8,128)S(1)}, f32[7,3,8,32,128]{4,3,2,1,0:T(8,128)S(1)}) custom-call(s32[7]{0:T(128)S(1)} %stack.55.edges, f32[3,8,16,128]{3,2,1,0:T(8,128)S(1)} %get-tuple-element.89.motion, f32[16,128]{1,0:T(8,128)S(1)} %collective-permute-done.9.z_low, f32[16,128]{1,0:T(8,128)S(1)} %collective-permute-done.10.z_high, ...), custom_call_target="tpu_custom_call" | custom-call | tf_op jit(solution)/shard_map/force_early/pallas_call | solution.py:791
  56.8 3.2 %collective-permute-start.13 = (f32[192,128]{1,0:T(8,128)S(1)}, f32[192,128]{1,0:T(8,128)S(1)}, u32[]{:S(2)}, u32[]{:S(2)}) collective-permute-start(f32[192,128]{1,0:T(8,128)S(1)} %get-tuple-element.103), channel_id=1, source_target_pairs={{0,224},{32,64},{64,32},{96,128},{128,96},{160,192},{192,160},{224... | collective-permute-start | bytes 294920 | tf_op jit(solution)/shard_map/ppermute | solution.py:819
  60.0 2.9 %force_late.4.inner = f32[3,8,16,128]{3,2,1,0:T(8,128)S(1)} custom-call(s32[7]{0:T(128)S(1)} %stack.55.edges, f32[3,8,16,128]{3,2,1,0:T(8,128)S(1)} %get-tuple-element.89.motion, f32[3,8,16,128]{3,2,1,0:T(8,128)S(1)} %get-tuple-element.99.early, f32[7,3,8,32,128]{4,3,2,1,0:T(8,128)S(1)} %get-tuple-element.100.early_shifts, ...), custom_call_target="tpu_custom_call" | custom-call | tf_op jit(solution)/shard_map/force_late/pallas_call | solution.py:791
  63.0 1.7 %finish_middle.1 = (f32[3,8,16,128]{3,2,1,0:T(8,128)S(1)}, f32[3,8,16,128]{3,2,1,0:T(8,128)S(1)}, f32[16,128]{1,0:T(8,128)S(1)}, f32[16,128]{1,0:T(8,128)S(1)}) custom-call(s32[7]{0:T(128)S(1)} %stack.55.edges, f32[3,8,16,128]{3,2,1,0:T(8,128)S(1)} %get-tuple-element.89.motion, f32[3,8,16,128]{3,2,1,0:T(8,128)S(1)} %get-tuple-element.90.speed, ...), custom_call_target="tpu_custom_call" | custom-call | tf_op jit(solution)/shard_map/finish_middle/pallas_call | solution.py:791
  64.8 1.5 %collective-permute-start.16 = (f32[16,128]{1,0:T(8,128)S(1)}, f32[16,128]{1,0:T(8,128)S(1)}, u32[]{:S(2)}, u32[]{:S(2)}) collective-permute-start(f32[16,128]{1,0:T(8,128)S(1)} %get-tuple-element.108), channel_id=1, source_target_pairs={{0,3},{1,0},{2,1},{3,2},{4,7},{5,4},{6,5},{7,6},{8,11},{9,8},{10,9... | collective-permute-start | bytes 24584 | tf_op jit(solution)/shard_map/ppermute | solution.py:813
  66.3 0.8 force_level.3.refs_0_
  67.3 1.5 %collective-permute-done.16.z_high = f32[16,128]{1,0:T(8,128)S(1)} collective-permute-done((f32[16,128]{1,0:T(8,128)S(1)}, f32[16,128]{1,0:T(8,128)S(1)}, u32[]{:S(2)}, u32[]{:S(2)}) %collective-permute-start.16) | collective-permute-done | bytes 8224 | tf_op jit(solution)/shard_map/ppermute | solution.py:813
  69.5 3.6 %collective-permute-start.18 = (f32[80,128]{1,0:T(8,128)S(1)}, f32[80,128]{1,0:T(8,128)S(1)}, u32[]{:S(2)}, u32[]{:S(2)}) collective-permute-start(f32[80,128]{1,0:T(8,128)S(1)} %get-tuple-element.112), channel_id=1, source_target_pairs={{0,28},{4,0},{8,4},{12,8},{16,12},{20,16},{24,20},{28,24},{1,29},{... | collective-permute-start | bytes 122888 | tf_op jit(solution)/shard_map/ppermute | solution.py:813
  73.1 3.3 %force_early.5 = (f32[3,8,16,128]{3,2,1,0:T(8,128)S(1)}, f32[7,3,8,32,128]{4,3,2,1,0:T(8,128)S(1)}) custom-call(s32[7]{0:T(128)S(1)} %stack.55.edges, f32[3,8,16,128]{3,2,1,0:T(8,128)S(1)} %get-tuple-element.105.motion, f32[16,128]{1,0:T(8,128)S(1)} %collective-permute-done.15.z_low, f32[16,128]{1,0:T(8,128)S(1)} %collective-permute-done.16.z_high, ...), custom_call_target="tpu_custom_call" | custom-call | tf_op jit(solution)/shard_map/force_early/pallas_call | solution.py:791
  77.0 4.9 %collective-permute-start.19 = (f32[192,128]{1,0:T(8,128)S(1)}, f32[192,128]{1,0:T(8,128)S(1)}, u32[]{:S(2)}, u32[]{:S(2)}) collective-permute-start(f32[192,128]{1,0:T(8,128)S(1)} %get-tuple-element.119), channel_id=1, source_target_pairs={{0,224},{32,64},{64,32},{96,128},{128,96},{160,192},{192,160},{224... | collective-permute-start | bytes 294920 | tf_op jit(solution)/shard_map/ppermute | solution.py:819
  81.9 2.9 %force_late.5.inner = f32[3,8,16,128]{3,2,1,0:T(8,128)S(1)} custom-call(s32[7]{0:T(128)S(1)} %stack.55.edges, f32[3,8,16,128]{3,2,1,0:T(8,128)S(1)} %get-tuple-element.105.motion, f32[3,8,16,128]{3,2,1,0:T(8,128)S(1)} %get-tuple-element.115.early, f32[7,3,8,32,128]{4,3,2,1,0:T(8,128)S(1)} %get-tuple-element.116.early_shifts, ...), custom_call_target="tpu_custom_call" | custom-call | tf_op jit(solution)/shard_map/force_late/pallas_call | solution.py:791
  84.9 2.3 %finish_last.1 = (f32[3,8,16,128]{3,2,1,0:T(8,128)}, f32[3,8,16,128]{3,2,1,0:T(8,128)}, f32[3,8,16,128]{3,2,1,0:T(8,128)}) custom-call(s32[7]{0:T(128)S(1)} %stack.55.edges, f32[3,8,16,128]{3,2,1,0:T(8,128)S(1)} %get-tuple-element.105.motion, f32[3,8,16,128]{3,2,1,0:T(8,128)S(1)} %get-tuple-element.106.speed, ...), custom_call_target="tpu_custom_call" | custom-call | tf_op jit(solution)/shard_map/finish_last/pallas_call | solution.py:791
  (34 shorter events, 6.0 us)
Async XLA Ops:
  4.5 26.1 %collective-permute-start.4 = (f32[1120,128]{1,0:T(8,128)S(1)}, f32[1120,128]{1,0:T(8,128)S(1)}, u32[]{:S(2)}, u32[]{:S(2)}) collective-permute-start(f32[1120,128]{1,0:T(8,128)S(1)} %get-tuple-element.69.x_up), channel_id=1, source_target_pairs={{0,32},{32,64},{64,96},{96,128},{128,160},{160,192},{192,224},{224... | collective-permute-start | bytes 1720328 | tf_op jit(solution)/shard_map/ppermute | solution.py:813
  9.3 21.3 %collective-permute-start.5 = (f32[368,128]{1,0:T(8,128)S(1)}, f32[368,128]{1,0:T(8,128)S(1)}, u32[]{:S(2)}, u32[]{:S(2)}) collective-permute-start(f32[368,128]{1,0:T(8,128)S(1)} %get-tuple-element.74), channel_id=1, source_target_pairs={{0,4},{4,8},{8,12},{12,16},{16,20},{20,24},{24,28},{28,0},{1,5},{5... | collective-permute-start | bytes 565256 | tf_op jit(solution)/shard_map/ppermute | solution.py:813
  10.1 4.4 %collective-permute-start = (f32[152,128]{1,0:T(8,128)S(1)}, f32[152,128]{1,0:T(8,128)S(1)}, u32[]{:S(2)}, u32[]{:S(2)}) collective-permute-start(f32[152,128]{1,0:T(8,128)S(1)} %get-tuple-element.65), channel_id=1, source_target_pairs={{0,1},{1,2},{2,3},{3,0},{4,5},{5,6},{6,7},{7,4},{8,9},{9,10},{10,1... | collective-permute-start | bytes 233480 | tf_op jit(solution)/shard_map/ppermute | solution.py:813
  10.3 4.6 %collective-permute-start.1 = (f32[152,128]{1,0:T(8,128)S(1)}, f32[152,128]{1,0:T(8,128)S(1)}, u32[]{:S(2)}, u32[]{:S(2)}) collective-permute-start(f32[152,128]{1,0:T(8,128)S(1)} %get-tuple-element.66), channel_id=1, source_target_pairs={{0,3},{1,0},{2,1},{3,2},{4,7},{5,4},{6,5},{7,6},{8,11},{9,8},{10,9... | collective-permute-start | bytes 233480 | tf_op jit(solution)/shard_map/ppermute | solution.py:813
  11.5 19.1 %collective-permute-start.6 = (f32[224,128]{1,0:T(8,128)S(1)}, f32[224,128]{1,0:T(8,128)S(1)}, u32[]{:S(2)}, u32[]{:S(2)}) collective-permute-start(f32[224,128]{1,0:T(8,128)S(1)} %get-tuple-element.75), channel_id=1, source_target_pairs={{0,28},{4,0},{8,4},{12,8},{16,12},{20,16},{24,20},{28,24},{1,29},{... | collective-permute-start | bytes 344072 | tf_op jit(solution)/shard_map/ppermute | solution.py:813
  15.5 14.2 %collective-permute-start.2 = (f32[176,128]{1,0:T(8,128)S(1)}, f32[176,128]{1,0:T(8,128)S(1)}, u32[]{:S(2)}, u32[]{:S(2)}) collective-permute-start(f32[176,128]{1,0:T(8,128)S(1)} %get-tuple-element.67), channel_id=1, source_target_pairs={{0,4},{4,8},{8,12},{12,16},{16,20},{20,24},{24,28},{28,0},{1,5},{5... | collective-permute-start | bytes 270344 | tf_op jit(solution)/shard_map/ppermute | solution.py:813
  17.3 13.3 %collective-permute-start.3 = (f32[176,128]{1,0:T(8,128)S(1)}, f32[176,128]{1,0:T(8,128)S(1)}, u32[]{:S(2)}, u32[]{:S(2)}) collective-permute-start(f32[176,128]{1,0:T(8,128)S(1)} %get-tuple-element.68), channel_id=1, source_target_pairs={{0,28},{4,0},{8,4},{12,8},{16,12},{20,16},{24,20},{28,24},{1,29},{... | collective-permute-start | bytes 270344 | tf_op jit(solution)/shard_map/ppermute | solution.py:813
  31.3 7.7 %collective-permute-start.7 = (f32[440,128]{1,0:T(8,128)S(1)}, f32[440,128]{1,0:T(8,128)S(1)}, u32[]{:S(2)}, u32[]{:S(2)}) collective-permute-start(f32[440,128]{1,0:T(8,128)S(1)} %get-tuple-element.79), channel_id=1, source_target_pairs={{0,224},{32,64},{64,32},{96,128},{128,96},{160,192},{192,160},{224... | collective-permute-start | bytes 675848 | tf_op jit(solution)/shard_map/ppermute | solution.py:819
  33.3 5.7 %collective-permute-start.8 = (f32[440,128]{1,0:T(8,128)S(1)}, f32[440,128]{1,0:T(8,128)S(1)}, u32[]{:S(2)}, u32[]{:S(2)}) collective-permute-start(f32[440,128]{1,0:T(8,128)S(1)} %get-tuple-element.80), channel_id=1, source_target_pairs={{0,32},{32,0},{64,96},{96,64},{128,160},{160,128},{192,224},{224,1... | collective-permute-start | bytes 675848 | tf_op jit(solution)/shard_map/ppermute | solution.py:820
  35.6 4.4 %copy-start = (f32[3,8,16,128]{3,2,1,0:T(8,128)S(1)}, f32[3,8,16,128]{3,2,1,0:T(8,128)}, u32[]{:S(2)}) copy-start(f32[3,8,16,128]{3,2,1,0:T(8,128)} %speed.1) | copy-start | bytes 589828
  41.7 2.6 %collective-permute-start.9 = (f32[16,128]{1,0:T(8,128)S(1)}, f32[16,128]{1,0:T(8,128)S(1)}, u32[]{:S(2)}, u32[]{:S(2)}) collective-permute-start(f32[16,128]{1,0:T(8,128)S(1)} %get-tuple-element.91), channel_id=1, source_target_pairs={{0,1},{1,2},{2,3},{3,0},{4,5},{5,6},{6,7},{7,4},{8,9},{9,10},{10,1... | collective-permute-start | bytes 24584 | tf_op jit(solution)/shard_map/ppermute | solution.py:813
  42.0 3.7 %collective-permute-start.10 = (f32[16,128]{1,0:T(8,128)S(1)}, f32[16,128]{1,0:T(8,128)S(1)}, u32[]{:S(2)}, u32[]{:S(2)}) collective-permute-start(f32[16,128]{1,0:T(8,128)S(1)} %get-tuple-element.92), channel_id=1, source_target_pairs={{0,3},{1,0},{2,1},{3,2},{4,7},{5,4},{6,5},{7,6},{8,11},{9,8},{10,9... | collective-permute-start | bytes 24584 | tf_op jit(solution)/shard_map/ppermute | solution.py:813
  46.3 9.8 %collective-permute-start.11 = (f32[80,128]{1,0:T(8,128)S(1)}, f32[80,128]{1,0:T(8,128)S(1)}, u32[]{:S(2)}, u32[]{:S(2)}) collective-permute-start(f32[80,128]{1,0:T(8,128)S(1)} %get-tuple-element.95), channel_id=1, source_target_pairs={{0,4},{4,8},{8,12},{12,16},{16,20},{20,24},{24,28},{28,0},{1,5},{5... | collective-permute-start | bytes 122888 | tf_op jit(solution)/shard_map/ppermute | solution.py:813
  50.6 5.5 %collective-permute-start.12 = (f32[80,128]{1,0:T(8,128)S(1)}, f32[80,128]{1,0:T(8,128)S(1)}, u32[]{:S(2)}, u32[]{:S(2)}) collective-permute-start(f32[80,128]{1,0:T(8,128)S(1)} %get-tuple-element.96), channel_id=1, source_target_pairs={{0,28},{4,0},{8,4},{12,8},{16,12},{20,16},{24,20},{28,24},{1,29},{... | collective-permute-start | bytes 122888 | tf_op jit(solution)/shard_map/ppermute | solution.py:813
  56.8 6.2 %collective-permute-start.13 = (f32[192,128]{1,0:T(8,128)S(1)}, f32[192,128]{1,0:T(8,128)S(1)}, u32[]{:S(2)}, u32[]{:S(2)}) collective-permute-start(f32[192,128]{1,0:T(8,128)S(1)} %get-tuple-element.103), channel_id=1, source_target_pairs={{0,224},{32,64},{64,32},{96,128},{128,96},{160,192},{192,160},{224... | collective-permute-start | bytes 294920 | tf_op jit(solution)/shard_map/ppermute | solution.py:819
  60.0 3.0 %collective-permute-start.14 = (f32[192,128]{1,0:T(8,128)S(1)}, f32[192,128]{1,0:T(8,128)S(1)}, u32[]{:S(2)}, u32[]{:S(2)}) collective-permute-start(f32[192,128]{1,0:T(8,128)S(1)} %get-tuple-element.104), channel_id=1, source_target_pairs={{0,32},{32,0},{64,96},{96,64},{128,160},{160,128},{192,224},{224,1... | collective-permute-start | bytes 294920 | tf_op jit(solution)/shard_map/ppermute | solution.py:820
  64.7 2.6 %collective-permute-start.15 = (f32[16,128]{1,0:T(8,128)S(1)}, f32[16,128]{1,0:T(8,128)S(1)}, u32[]{:S(2)}, u32[]{:S(2)}) collective-permute-start(f32[16,128]{1,0:T(8,128)S(1)} %get-tuple-element.107), channel_id=1, source_target_pairs={{0,1},{1,2},{2,3},{3,0},{4,5},{5,6},{6,7},{7,4},{8,9},{9,10},{10,1... | collective-permute-start | bytes 24584 | tf_op jit(solution)/shard_map/ppermute | solution.py:813
  64.8 4.0 %collective-permute-start.16 = (f32[16,128]{1,0:T(8,128)S(1)}, f32[16,128]{1,0:T(8,128)S(1)}, u32[]{:S(2)}, u32[]{:S(2)}) collective-permute-start(f32[16,128]{1,0:T(8,128)S(1)} %get-tuple-element.108), channel_id=1, source_target_pairs={{0,3},{1,0},{2,1},{3,2},{4,7},{5,4},{6,5},{7,6},{8,11},{9,8},{10,9... | collective-permute-start | bytes 24584 | tf_op jit(solution)/shard_map/ppermute | solution.py:813
  69.4 7.0 %collective-permute-start.17 = (f32[80,128]{1,0:T(8,128)S(1)}, f32[80,128]{1,0:T(8,128)S(1)}, u32[]{:S(2)}, u32[]{:S(2)}) collective-permute-start(f32[80,128]{1,0:T(8,128)S(1)} %get-tuple-element.111), channel_id=1, source_target_pairs={{0,4},{4,8},{8,12},{12,16},{16,20},{20,24},{24,28},{28,0},{1,5},{5... | collective-permute-start | bytes 122888 | tf_op jit(solution)/shard_map/ppermute | solution.py:813
  69.5 6.9 %collective-permute-start.18 = (f32[80,128]{1,0:T(8,128)S(1)}, f32[80,128]{1,0:T(8,128)S(1)}, u32[]{:S(2)}, u32[]{:S(2)}) collective-permute-start(f32[80,128]{1,0:T(8,128)S(1)} %get-tuple-element.112), channel_id=1, source_target_pairs={{0,28},{4,0},{8,4},{12,8},{16,12},{20,16},{24,20},{28,24},{1,29},{... | collective-permute-start | bytes 122888 | tf_op jit(solution)/shard_map/ppermute | solution.py:813
  77.0 7.8 %collective-permute-start.19 = (f32[192,128]{1,0:T(8,128)S(1)}, f32[192,128]{1,0:T(8,128)S(1)}, u32[]{:S(2)}, u32[]{:S(2)}) collective-permute-start(f32[192,128]{1,0:T(8,128)S(1)} %get-tuple-element.119), channel_id=1, source_target_pairs={{0,224},{32,64},{64,32},{96,128},{128,96},{160,192},{192,160},{224... | collective-permute-start | bytes 294920 | tf_op jit(solution)/shard_map/ppermute | solution.py:819
  81.9 2.9 %collective-permute-start.20 = (f32[192,128]{1,0:T(8,128)S(1)}, f32[192,128]{1,0:T(8,128)S(1)}, u32[]{:S(2)}, u32[]{:S(2)}) collective-permute-start(f32[192,128]{1,0:T(8,128)S(1)} %get-tuple-element.120), channel_id=1, source_target_pairs={{0,32},{32,0},{64,96},{96,64},{128,160},{160,128},{192,224},{224,1... | collective-permute-start | bytes 294920 | tf_op jit(solution)/shard_map/ppermute | solution.py:820
